TPU v7x, 32 devices: a whole 2x2x4 slice. The times are simulated.
32 devices in a mesh: tx: 8 (over z, core), gx: 2 (over x), gy: 2 (over y).
Axes of the slice: x: 2, y: 2, z: 4, core: 2. Of those that a mesh axis runs over, the one named last changes fastest.
Arguments:
- cond_h: float32 [32, 32, 128], P('gx', 'gy'), may hold values from 0.1 to 1.5
- cond_v: float32 [32, 32, 128], P('gx', 'gy'), may hold values from 0.1 to 1.5
- fwd_init: float32 [8, 6, 32, 32, 128], P('tx', None, 'gx', 'gy'), may hold values from -6 to 6
- adj_init: float32 [8, 6, 32, 32, 128], P('tx', None, 'gx', 'gy'), may hold values from -6 to 6
- observed: float32 [8, 4, 2, 2, 2, 32], P('tx', None, 'gx', 'gy'), may hold values from -6 to 6
- footprint: int32 [8, 2, 2], P('tx', 'gx', 'gy'), may hold values 0 or 1
- owner: int32 [2, 2, 8], P('gx', 'gy'), may hold values from 0 to 7, each once within a row
- rec_cells: int32 [2, 2, 32], P('gx', 'gy'), may hold values from 0 to 255
Outputs:
- owned_gradient: float32 [2, 8, 2, 2, 32, 128], P('gx', 'tx', None, None, 'gy')
- misfit: float32 [], replicated
Inputs may be any that keep to these rules, and one draw needn't show every extreme that they name: `owner`: each tile's row is a permutation of 0 to 7. `rec_cells`: cell index x * 16 + y within the tile; receivers may share a cell. `footprint`: 1 where the group's gradient counts in the tile.
All inputs are finite; a program needn't handle non-finite values.
Results may differ from a plain program's by a relative error of at most 0.00028.
Values sent between devices are 32-bit elements; how exact they have to be, the bound alone decides.
A program may use at most 64 MiB of HBM per device.

v0:
```python
import jax
import jax.numpy as jnp
from jax import lax
from jax.sharding import PartitionSpec as P

STEPS = 4
ZREC = 32


STEP_DT = 0.5


def shifted(x, axis, by):
    size = lax.axis_size(axis)
    pairs = [(i, i + by) for i in range(size) if 0 <= i + by < size]
    return lax.ppermute(x, axis, pairs)


def coefficients(conduct):
    half_rate = 0.25 * conduct
    return ((1.0 - half_rate) / (1.0 + half_rate), STEP_DT / (1.0 + half_rate))


def ahead_of(values, tail_plane, axis_num):
    extent = values.shape[axis_num]
    return jnp.concatenate(
        [lax.slice_in_dim(values, 1, extent, axis=axis_num), tail_plane], axis=axis_num
    )


def before(values, head_plane, axis_num):
    extent = values.shape[axis_num]
    return jnp.concatenate(
        [head_plane, lax.slice_in_dim(values, 0, extent - 1, axis=axis_num)], axis=axis_num
    )


def zero_plane(values, axis_num):
    return jnp.zeros_like(lax.slice_in_dim(values, 0, 1, axis=axis_num))


def curl_ahead(field, next_x, next_y):
    comp_x, comp_y, comp_z = (field[0], field[1], field[2])
    out_x = (
        ahead_of(comp_z, next_y[1], 1)
        - comp_z
        - (ahead_of(comp_y, zero_plane(comp_y, 2), 2) - comp_y)
    )
    out_y = (
        ahead_of(comp_x, zero_plane(comp_x, 2), 2)
        - comp_x
        - (ahead_of(comp_z, next_x[1], 0) - comp_z)
    )
    out_z = ahead_of(comp_y, next_x[0], 0) - comp_y - (ahead_of(comp_x, next_y[0], 1) - comp_x)
    return jnp.stack([out_x, out_y, out_z])


def curl_before(field, prev_x, prev_y):
    comp_x, comp_y, comp_z = (field[0], field[1], field[2])
    out_x = (
        comp_z - before(comp_z, prev_y[1], 1) - (comp_y - before(comp_y, zero_plane(comp_y, 2), 2))
    )
    out_y = (
        comp_x - before(comp_x, zero_plane(comp_x, 2), 2) - (comp_z - before(comp_z, prev_x[1], 0))
    )
    out_z = comp_y - before(comp_y, prev_x[0], 0) - (comp_x - before(comp_x, prev_y[0], 1))
    return jnp.stack([out_x, out_y, out_z])


def electric_rims(electric):
    next_x = shifted(electric[1:3, 0:1], "gx", -1)
    next_y = shifted(electric[0::2, :, 0:1], "gy", -1)
    return (next_x, next_y)


def magnetic_rims(magnetic):
    size_x = magnetic.shape[1]
    size_y = magnetic.shape[2]
    prev_x = shifted(magnetic[1:3, size_x - 1 : size_x], "gx", 1)
    prev_y = shifted(magnetic[0::2, :, size_y - 1 : size_y], "gy", 1)
    return (prev_x, prev_y)


def advance(electric, magnetic, decay, drive):
    next_x, next_y = electric_rims(electric)
    magnetic = magnetic - STEP_DT * curl_ahead(electric, next_x, next_y)
    prev_x, prev_y = magnetic_rims(magnetic)
    electric = decay * electric + drive * curl_before(magnetic, prev_x, prev_y)
    return (electric, magnetic)


def on_device(cond_h, cond_v, fwd_init, adj_init, observed, footprint, owner, rec_cells):
    size_x, size_y, depth = cond_h.shape
    decay_h, drive_h = coefficients(cond_h)
    decay_v, drive_v = coefficients(cond_v)
    highest = lax.Precision.HIGHEST
    cell_ids = jnp.arange(size_x * size_y, dtype=jnp.int32)
    onehot = (rec_cells[0, 0][:, None] == cell_ids[None, :]).astype(jnp.float32)
    observe = observed[0, :, 0, 0]
    grad_h = jnp.zeros((size_x, size_y, depth), jnp.float32)
    grad_v = jnp.zeros((size_x, size_y, depth), jnp.float32)
    residuals = []
    decay = jnp.stack([decay_h, decay_h, decay_v])
    drive = jnp.stack([drive_h, drive_h, drive_v])
    electric, magnetic = (fwd_init[0, 0:3], fwd_init[0, 3:6])
    stored = []
    for step_idx in range(STEPS):
        electric, magnetic = advance(electric, magnetic, decay, drive)
        stored.append(electric)
        planes = electric[0:2, :, :, ZREC].reshape(2, size_x * size_y)
        residuals.append(jnp.dot(planes, onehot.T, precision=highest) - observe[step_idx])
    adj_e, adj_h = (adj_init[0, 0:3], adj_init[0, 3:6])
    for step_idx in reversed(range(STEPS)):
        adj_e = adj_e.at[0:2, :, :, ZREC].add(
            jnp.dot(residuals[step_idx], onehot, precision=highest).reshape(2, size_x, size_y)
        )
        adj_e, adj_h = advance(adj_e, adj_h, decay, drive)
        kept = stored[step_idx]
        grad_h = grad_h + adj_e[0] * kept[0] + adj_e[1] * kept[1]
        grad_v = grad_v + adj_e[2] * kept[2]
    local_misfit = jnp.float32(0.0)
    for step_idx in range(STEPS):
        local_misfit = local_misfit + 0.5 * jnp.sum(residuals[step_idx] * residuals[step_idx])
    misfit = lax.psum(local_misfit, ("tx", "gx", "gy"))
    tile_flag = footprint[0, 0, 0].astype(jnp.float32)
    gradient = jnp.stack([grad_h, grad_v]) * tile_flag
    groups_count = lax.axis_size("tx")
    block_rows = size_x // groups_count
    blocked = gradient.reshape(2, groups_count, block_rows, size_y, depth)
    ordered = jnp.take(blocked, owner[0, 0], axis=1)
    summed = lax.psum_scatter(ordered, "tx", scatter_dimension=1, tiled=True)
    owned_part = summed.reshape(1, 1, 2, block_rows, size_y, depth)
    return (owned_part, misfit)


def solution(mesh):
    placed = (
        P("gx", "gy", None),
        P("gx", "gy", None),
        P("tx", None, "gx", "gy", None),
        P("tx", None, "gx", "gy", None),
        P("tx", None, "gx", "gy", None, None),
        P("tx", "gx", "gy"),
        P("gx", "gy", None),
        P("gx", "gy", None),
    )
    return jax.shard_map(
        on_device,
        mesh=mesh,
        in_specs=placed,
        out_specs=(P("gx", "tx", None, None, "gy", None), P()),
        check_vma=False,
    )
```

profile of v0, /device:TPU:1, one launch (start us, length us, event | category | flops | bytes accessed | tf_op | source)
XLA Modules:
  0.0 251.8 jit_solution(8642202150219873762)
XLA Ops:
  15.4 2.0 and_reduce_fusion
  19.2 4.0 %collective-permute-start.2 = (f32[2,16,1,128]{3,1,2,0:T(8,128)S(1)}, f32[2,16,1,128]{3,1,2,0:T(8,128)S(1)}, u32[]{:S(2)}, u32[]{:S(2)}) collective-permute-start(f32[2,16,1,128]{3,1,2,0:T(8,128)S(1)} %bitcast.587), channel_id=1, source_target_pairs={{0,1},{2,3},{4,5},{6,7},{8,9},{10,11},{12,13},{14,15},{16,17},{18,... | collective-permute-start | bytes 49160 | tf_op jit(solution)/shard_map/ppermute | solution.py:16
  23.2 4.0 %collective-permute-start.3 = (f32[2,1,16,128]{3,2,1,0:T(8,128)S(1)}, f32[2,1,16,128]{3,2,1,0:T(8,128)S(1)}, u32[]{:S(2)}, u32[]{:S(2)}) collective-permute-start(f32[2,1,16,128]{3,2,1,0:T(8,128)S(1)} %slice.1340), channel_id=1, source_target_pairs={{0,2},{1,3},{4,6},{5,7},{8,10},{9,11},{12,14},{13,15},{16,18},{17,... | collective-permute-start | bytes 49160 | tf_op jit(solution)/shard_map/ppermute | solution.py:16
  38.2 4.0 %collective-permute-start.6 = (f32[2,16,1,128]{3,1,2,0:T(8,128)S(1)}, f32[2,16,1,128]{3,1,2,0:T(8,128)S(1)}, u32[]{:S(2)}, u32[]{:S(2)}) collective-permute-start(f32[2,16,1,128]{3,1,2,0:T(8,128)S(1)} %bitcast.588), channel_id=1, source_target_pairs={{0,1},{2,3},{4,5},{6,7},{8,9},{10,11},{12,13},{14,15},{16,17},{18,... | collective-permute-start | bytes 49160 | tf_op jit(solution)/shard_map/ppermute | solution.py:16
  42.2 4.0 %collective-permute-start.7 = (f32[2,1,16,128]{3,2,1,0:T(8,128)S(1)}, f32[2,1,16,128]{3,2,1,0:T(8,128)S(1)}, u32[]{:S(2)}, u32[]{:S(2)}) collective-permute-start(f32[2,1,16,128]{3,2,1,0:T(8,128)S(1)} %slice.1368), channel_id=1, source_target_pairs={{0,2},{1,3},{4,6},{5,7},{8,10},{9,11},{12,14},{13,15},{16,18},{17,... | collective-permute-start | bytes 49160 | tf_op jit(solution)/shard_map/ppermute | solution.py:16
  61.6 4.0 %collective-permute-start.10 = (f32[2,16,1,128]{3,1,2,0:T(8,128)S(1)}, f32[2,16,1,128]{3,1,2,0:T(8,128)S(1)}, u32[]{:S(2)}, u32[]{:S(2)}) collective-permute-start(f32[2,16,1,128]{3,1,2,0:T(8,128)S(1)} %bitcast.589), channel_id=1, source_target_pairs={{0,1},{2,3},{4,5},{6,7},{8,9},{10,11},{12,13},{14,15},{16,17},{18,... | collective-permute-start | bytes 49160 | tf_op jit(solution)/shard_map/ppermute | solution.py:16
  65.6 1.9 collective-permute-start.11
  85.8 4.6 %collective-permute-start.14 = (f32[2,16,1,128]{3,1,2,0:T(8,128)S(1)}, f32[2,16,1,128]{3,1,2,0:T(8,128)S(1)}, u32[]{:S(2)}, u32[]{:S(2)}) collective-permute-start(f32[2,16,1,128]{3,1,2,0:T(8,128)S(1)} %bitcast.590), channel_id=1, source_target_pairs={{0,1},{2,3},{4,5},{6,7},{8,9},{10,11},{12,13},{14,15},{16,17},{18,... | collective-permute-start | bytes 49160 | tf_op jit(solution)/shard_map/ppermute | solution.py:16
  90.4 4.3 %collective-permute-start.15 = (f32[2,1,16,128]{3,2,1,0:T(8,128)S(1)}, f32[2,1,16,128]{3,2,1,0:T(8,128)S(1)}, u32[]{:S(2)}, u32[]{:S(2)}) collective-permute-start(f32[2,1,16,128]{3,2,1,0:T(8,128)S(1)} %slice.1424), channel_id=1, source_target_pairs={{0,2},{1,3},{4,6},{5,7},{8,10},{9,11},{12,14},{13,15},{16,18},{17,... | collective-permute-start | bytes 49160 | tf_op jit(solution)/shard_map/ppermute | solution.py:16
  100.0 2.0 add_select_fusion.3
  102.1 3.6 %scatter-add.14 = f32[3,16,16,128]{3,2,1,0:T(8,128)S(1)} dynamic-update-slice(f32[3,16,16,128]{3,2,1,0:T(8,128)S(1)} %get-tuple-element.51, f32[2,16,16,1]{3,2,1,0:T(8,128)S(1)} %add_select_fusion.3, s32[]{:T(128)} %bitcast.4, s32[]{:T(128)} %constant.106.clone.1, s32[]{:T(128)} %constant.106.clone.1, s32[]{:T(128)} %bitcast.5) | dynamic-update-slice | bytes 4100 | tf_op jit(solution)/shard_map/scatter-add | solution.py:114
  108.5 1.7 collective-permute-done.16
  113.0 4.0 %collective-permute-start.18 = (f32[2,16,1,128]{3,1,2,0:T(8,128)S(1)}, f32[2,16,1,128]{3,1,2,0:T(8,128)S(1)}, u32[]{:S(2)}, u32[]{:S(2)}) collective-permute-start(f32[2,16,1,128]{3,1,2,0:T(8,128)S(1)} %bitcast.591), channel_id=1, source_target_pairs={{0,1},{2,3},{4,5},{6,7},{8,9},{10,11},{12,13},{14,15},{16,17},{18,... | collective-permute-start | bytes 49160 | tf_op jit(solution)/shard_map/ppermute | solution.py:16
  120.9 2.0 add_select_fusion.2
  122.9 3.6 %scatter-add.15 = f32[3,16,16,128]{3,2,1,0:T(8,128)S(1)} dynamic-update-slice(f32[3,16,16,128]{3,2,1,0:T(8,128)S(1)} %copy.84, f32[2,16,16,1]{3,2,1,0:T(8,128)S(1)} %add_select_fusion.2, s32[]{:T(128)} %bitcast.4, s32[]{:T(128)} %constant.106.clone.1, s32[]{:T(128)} %constant.106.clone.1, s32[]{:T(128)} %bitcast.5) | dynamic-update-slice | bytes 4100 | tf_op jit(solution)/shard_map/scatter-add | solution.py:114
  129.3 1.7 collective-permute-done.20
  134.0 4.0 %collective-permute-start.22 = (f32[2,16,1,128]{3,1,2,0:T(8,128)S(1)}, f32[2,16,1,128]{3,1,2,0:T(8,128)S(1)}, u32[]{:S(2)}, u32[]{:S(2)}) collective-permute-start(f32[2,16,1,128]{3,1,2,0:T(8,128)S(1)} %bitcast.592), channel_id=1, source_target_pairs={{0,1},{2,3},{4,5},{6,7},{8,9},{10,11},{12,13},{14,15},{16,17},{18,... | collective-permute-start | bytes 49160 | tf_op jit(solution)/shard_map/ppermute | solution.py:16
  141.8 2.0 add_select_fusion.1
  143.9 3.6 %scatter-add.16 = f32[3,16,16,128]{3,2,1,0:T(8,128)S(1)} dynamic-update-slice(f32[3,16,16,128]{3,2,1,0:T(8,128)S(1)} %copy.85, f32[2,16,16,1]{3,2,1,0:T(8,128)S(1)} %add_select_fusion.1, s32[]{:T(128)} %bitcast.4, s32[]{:T(128)} %constant.106.clone.1, s32[]{:T(128)} %constant.106.clone.1, s32[]{:T(128)} %bitcast.5) | dynamic-update-slice | bytes 4100 | tf_op jit(solution)/shard_map/scatter-add | solution.py:114
  155.1 4.0 %collective-permute-start.26 = (f32[2,16,1,128]{3,1,2,0:T(8,128)S(1)}, f32[2,16,1,128]{3,1,2,0:T(8,128)S(1)}, u32[]{:S(2)}, u32[]{:S(2)}) collective-permute-start(f32[2,16,1,128]{3,1,2,0:T(8,128)S(1)} %bitcast.593), channel_id=1, source_target_pairs={{0,1},{2,3},{4,5},{6,7},{8,9},{10,11},{12,13},{14,15},{16,17},{18,... | collective-permute-start | bytes 49160 | tf_op jit(solution)/shard_map/ppermute | solution.py:16
  163.1 2.0 add_select_fusion
  165.2 3.6 %scatter-add.19 = f32[3,16,16,128]{3,2,1,0:T(8,128)S(1)} dynamic-update-slice(f32[3,16,16,128]{3,2,1,0:T(8,128)S(1)} %copy.86, f32[2,16,16,1]{3,2,1,0:T(8,128)S(1)} %add_select_fusion, s32[]{:T(128)} %bitcast.4, s32[]{:T(128)} %constant.106.clone.1, s32[]{:T(128)} %constant.106.clone.1, s32[]{:T(128)} %bitcast.5) | dynamic-update-slice | bytes 4100 | tf_op jit(solution)/shard_map/scatter-add | solution.py:114
  176.5 4.0 %collective-permute-start.30 = (f32[2,16,1,128]{3,1,2,0:T(8,128)S(1)}, f32[2,16,1,128]{3,1,2,0:T(8,128)S(1)}, u32[]{:S(2)}, u32[]{:S(2)}) collective-permute-start(f32[2,16,1,128]{3,1,2,0:T(8,128)S(1)} %bitcast.594), channel_id=1, source_target_pairs={{0,1},{2,3},{4,5},{6,7},{8,9},{10,11},{12,13},{14,15},{16,17},{18,... | collective-permute-start | bytes 49160 | tf_op jit(solution)/shard_map/ppermute | solution.py:16
  188.7 56.3 %psum.7 = f32[]{:T(128)} all-reduce(f32[]{:T(128)S(6)} %add.229), channel_id=1, replica_groups=mesh['tx'=8,'gx'=2,'gy'=2] {'tx','gx','gy'}, use_global_device_ids=true, to_apply=%region_6.0 | all-reduce | flops 1 | bytes 8 | tf_op jit(solution)/shard_map/psum | solution.py:124
  (437 shorter events, 101.4 us)
Async XLA Ops:
  7.2 237.8 %reduce-scatter.2.cloned.1.call-start = ((), (), s32[]{:S(2)}) async-start(), calls=%async_computation.1 | async-start | bytes 294912 | tf_op jit(solution)/shard_map/reduce_scatter | solution.py:131
  8.3 10.5 %collective-permute-start = (f32[2,16,1,128]{3,2,1,0:T(1,128)S(1)}, f32[2,16,1,128]{3,2,1,0:T(1,128)S(1)}, u32[]{:S(2)}, u32[]{:S(2)}) collective-permute-start(f32[2,16,1,128]{3,2,1,0:T(1,128)S(1)} %slice.1044), channel_id=1, source_target_pairs={{1,0},{3,2},{5,4},{7,6},{9,8},{11,10},{13,12},{15,14},{17,16},{19,... | collective-permute-start | bytes 49160 | tf_op jit(solution)/shard_map/ppermute | solution.py:16
  9.6 9.2 %collective-permute-start.1 = (f32[2,1,16,128]{3,2,1,0:T(8,128)S(1)}, f32[2,1,16,128]{3,2,1,0:T(8,128)S(1)}, u32[]{:S(2)}, u32[]{:S(2)}) collective-permute-start(f32[2,1,16,128]{3,2,1,0:T(8,128)S(1)} %slice.1328), channel_id=1, source_target_pairs={{2,0},{3,1},{6,4},{7,5},{10,8},{11,9},{14,12},{15,13},{18,16},{19,... | collective-permute-start | bytes 49160 | tf_op jit(solution)/shard_map/ppermute | solution.py:16
  19.2 8.0 %collective-permute-start.2 = (f32[2,16,1,128]{3,1,2,0:T(8,128)S(1)}, f32[2,16,1,128]{3,1,2,0:T(8,128)S(1)}, u32[]{:S(2)}, u32[]{:S(2)}) collective-permute-start(f32[2,16,1,128]{3,1,2,0:T(8,128)S(1)} %bitcast.587), channel_id=1, source_target_pairs={{0,1},{2,3},{4,5},{6,7},{8,9},{10,11},{12,13},{14,15},{16,17},{18,... | collective-permute-start | bytes 49160 | tf_op jit(solution)/shard_map/ppermute | solution.py:16
  23.2 4.8 %collective-permute-start.3 = (f32[2,1,16,128]{3,2,1,0:T(8,128)S(1)}, f32[2,1,16,128]{3,2,1,0:T(8,128)S(1)}, u32[]{:S(2)}, u32[]{:S(2)}) collective-permute-start(f32[2,1,16,128]{3,2,1,0:T(8,128)S(1)} %slice.1340), channel_id=1, source_target_pairs={{0,2},{1,3},{4,6},{5,7},{8,10},{9,11},{12,14},{13,15},{16,18},{17,... | collective-permute-start | bytes 49160 | tf_op jit(solution)/shard_map/ppermute | solution.py:16
  30.3 6.0 %collective-permute-start.4 = (f32[2,16,1,128]{3,2,1,0:T(1,128)S(1)}, f32[2,16,1,128]{3,2,1,0:T(1,128)S(1)}, u32[]{:S(2)}, u32[]{:S(2)}) collective-permute-start(f32[2,16,1,128]{3,2,1,0:T(1,128)S(1)} %slice.1076), channel_id=1, source_target_pairs={{1,0},{3,2},{5,4},{7,6},{9,8},{11,10},{13,12},{15,14},{17,16},{19,... | collective-permute-start | bytes 49160 | tf_op jit(solution)/shard_map/ppermute | solution.py:16
  31.6 4.7 %collective-permute-start.5 = (f32[2,1,16,128]{3,2,1,0:T(8,128)S(1)}, f32[2,1,16,128]{3,2,1,0:T(8,128)S(1)}, u32[]{:S(2)}, u32[]{:S(2)}) collective-permute-start(f32[2,1,16,128]{3,2,1,0:T(8,128)S(1)} %slice.1355), channel_id=1, source_target_pairs={{2,0},{3,1},{6,4},{7,5},{10,8},{11,9},{14,12},{15,13},{18,16},{19,... | collective-permute-start | bytes 49160 | tf_op jit(solution)/shard_map/ppermute | solution.py:16
  38.2 8.0 %collective-permute-start.6 = (f32[2,16,1,128]{3,1,2,0:T(8,128)S(1)}, f32[2,16,1,128]{3,1,2,0:T(8,128)S(1)}, u32[]{:S(2)}, u32[]{:S(2)}) collective-permute-start(f32[2,16,1,128]{3,1,2,0:T(8,128)S(1)} %bitcast.588), channel_id=1, source_target_pairs={{0,1},{2,3},{4,5},{6,7},{8,9},{10,11},{12,13},{14,15},{16,17},{18,... | collective-permute-start | bytes 49160 | tf_op jit(solution)/shard_map/ppermute | solution.py:16
  42.2 4.8 %collective-permute-start.7 = (f32[2,1,16,128]{3,2,1,0:T(8,128)S(1)}, f32[2,1,16,128]{3,2,1,0:T(8,128)S(1)}, u32[]{:S(2)}, u32[]{:S(2)}) collective-permute-start(f32[2,1,16,128]{3,2,1,0:T(8,128)S(1)} %slice.1368), channel_id=1, source_target_pairs={{0,2},{1,3},{4,6},{5,7},{8,10},{9,11},{12,14},{13,15},{16,18},{17,... | collective-permute-start | bytes 49160 | tf_op jit(solution)/shard_map/ppermute | solution.py:16
  53.8 4.5 %collective-permute-start.9 = (f32[2,1,16,128]{3,2,1,0:T(8,128)S(1)}, f32[2,1,16,128]{3,2,1,0:T(8,128)S(1)}, u32[]{:S(2)}, u32[]{:S(2)}) collective-permute-start(f32[2,1,16,128]{3,2,1,0:T(8,128)S(1)} %copy-done.72), channel_id=1, source_target_pairs={{2,0},{3,1},{6,4},{7,5},{10,8},{11,9},{14,12},{15,13},{18,16},{19,... | collective-permute-start | bytes 49160 | tf_op jit(solution)/shard_map/ppermute | solution.py:16
  61.6 6.0 %collective-permute-start.10 = (f32[2,16,1,128]{3,1,2,0:T(8,128)S(1)}, f32[2,16,1,128]{3,1,2,0:T(8,128)S(1)}, u32[]{:S(2)}, u32[]{:S(2)}) collective-permute-start(f32[2,16,1,128]{3,1,2,0:T(8,128)S(1)} %bitcast.589), channel_id=1, source_target_pairs={{0,1},{2,3},{4,5},{6,7},{8,9},{10,11},{12,13},{14,15},{16,17},{18,... | collective-permute-start | bytes 49160 | tf_op jit(solution)/shard_map/ppermute | solution.py:16
  75.6 5.1 %collective-permute-start.12 = (f32[2,16,1,128]{3,2,1,0:T(1,128)}, f32[2,16,1,128]{3,2,1,0:T(1,128)}, u32[]{:S(2)}, u32[]{:S(2)}) collective-permute-start(f32[2,16,1,128]{3,2,1,0:T(1,128)} %slice.1140), channel_id=1, source_target_pairs={{1,0},{3,2},{5,4},{7,6},{9,8},{11,10},{13,12},{15,14},{17,16},{19,... | collective-permute-start | bytes 49160 | tf_op jit(solution)/shard_map/ppermute | solution.py:16
  77.0 4.6 %collective-permute-start.13 = (f32[2,1,16,128]{3,2,1,0:T(8,128)S(1)}, f32[2,1,16,128]{3,2,1,0:T(8,128)}, u32[]{:S(2)}, u32[]{:S(2)}) collective-permute-start(f32[2,1,16,128]{3,2,1,0:T(8,128)S(1)} %copy-done.73), channel_id=1, source_target_pairs={{2,0},{3,1},{6,4},{7,5},{10,8},{11,9},{14,12},{15,13},{18,16},{19,... | collective-permute-start | bytes 49160 | tf_op jit(solution)/shard_map/ppermute | solution.py:16
  85.8 9.0 %collective-permute-start.14 = (f32[2,16,1,128]{3,1,2,0:T(8,128)S(1)}, f32[2,16,1,128]{3,1,2,0:T(8,128)S(1)}, u32[]{:S(2)}, u32[]{:S(2)}) collective-permute-start(f32[2,16,1,128]{3,1,2,0:T(8,128)S(1)} %bitcast.590), channel_id=1, source_target_pairs={{0,1},{2,3},{4,5},{6,7},{8,9},{10,11},{12,13},{14,15},{16,17},{18,... | collective-permute-start | bytes 49160 | tf_op jit(solution)/shard_map/ppermute | solution.py:16
  90.4 5.2 %collective-permute-start.15 = (f32[2,1,16,128]{3,2,1,0:T(8,128)S(1)}, f32[2,1,16,128]{3,2,1,0:T(8,128)S(1)}, u32[]{:S(2)}, u32[]{:S(2)}) collective-permute-start(f32[2,1,16,128]{3,2,1,0:T(8,128)S(1)} %slice.1424), channel_id=1, source_target_pairs={{0,2},{1,3},{4,6},{5,7},{8,10},{9,11},{12,14},{13,15},{16,18},{17,... | collective-permute-start | bytes 49160 | tf_op jit(solution)/shard_map/ppermute | solution.py:16
  105.7 4.5 %collective-permute-start.16 = (f32[2,16,1,128]{3,1,2,0:T(8,128)S(1)}, f32[2,16,1,128]{3,1,2,0:T(8,128)S(1)}, u32[]{:S(2)}, u32[]{:S(2)}) collective-permute-start(f32[2,16,1,128]{3,1,2,0:T(8,128)S(1)} %bitcast.584), channel_id=1, source_target_pairs={{1,0},{3,2},{5,4},{7,6},{9,8},{11,10},{13,12},{15,14},{17,16},{19,... | collective-permute-start | bytes 49160 | tf_op jit(solution)/shard_map/ppermute | solution.py:16
  107.2 4.5 %collective-permute-start.17 = (f32[2,1,16,128]{3,2,1,0:T(8,128)S(1)}, f32[2,1,16,128]{3,2,1,0:T(8,128)S(1)}, u32[]{:S(2)}, u32[]{:S(2)}) collective-permute-start(f32[2,1,16,128]{3,2,1,0:T(8,128)S(1)} %slice.1440), channel_id=1, source_target_pairs={{2,0},{3,1},{6,4},{7,5},{10,8},{11,9},{14,12},{15,13},{18,16},{19,... | collective-permute-start | bytes 49160 | tf_op jit(solution)/shard_map/ppermute | solution.py:16
  113.0 5.7 %collective-permute-start.18 = (f32[2,16,1,128]{3,1,2,0:T(8,128)S(1)}, f32[2,16,1,128]{3,1,2,0:T(8,128)S(1)}, u32[]{:S(2)}, u32[]{:S(2)}) collective-permute-start(f32[2,16,1,128]{3,1,2,0:T(8,128)S(1)} %bitcast.591), channel_id=1, source_target_pairs={{0,1},{2,3},{4,5},{6,7},{8,9},{10,11},{12,13},{14,15},{16,17},{18,... | collective-permute-start | bytes 49160 | tf_op jit(solution)/shard_map/ppermute | solution.py:16
  126.6 4.5 %collective-permute-start.20 = (f32[2,16,1,128]{3,1,2,0:T(8,128)S(1)}, f32[2,16,1,128]{3,1,2,0:T(8,128)S(1)}, u32[]{:S(2)}, u32[]{:S(2)}) collective-permute-start(f32[2,16,1,128]{3,1,2,0:T(8,128)S(1)} %bitcast.585), channel_id=1, source_target_pairs={{1,0},{3,2},{5,4},{7,6},{9,8},{11,10},{13,12},{15,14},{17,16},{19,... | collective-permute-start | bytes 49160 | tf_op jit(solution)/shard_map/ppermute | solution.py:16
  128.0 4.5 %collective-permute-start.21 = (f32[2,1,16,128]{3,2,1,0:T(8,128)S(1)}, f32[2,1,16,128]{3,2,1,0:T(8,128)S(1)}, u32[]{:S(2)}, u32[]{:S(2)}) collective-permute-start(f32[2,1,16,128]{3,2,1,0:T(8,128)S(1)} %slice.1473), channel_id=1, source_target_pairs={{2,0},{3,1},{6,4},{7,5},{10,8},{11,9},{14,12},{15,13},{18,16},{19,... | collective-permute-start | bytes 49160 | tf_op jit(solution)/shard_map/ppermute | solution.py:16
  134.0 5.7 %collective-permute-start.22 = (f32[2,16,1,128]{3,1,2,0:T(8,128)S(1)}, f32[2,16,1,128]{3,1,2,0:T(8,128)S(1)}, u32[]{:S(2)}, u32[]{:S(2)}) collective-permute-start(f32[2,16,1,128]{3,1,2,0:T(8,128)S(1)} %bitcast.592), channel_id=1, source_target_pairs={{0,1},{2,3},{4,5},{6,7},{8,9},{10,11},{12,13},{14,15},{16,17},{18,... | collective-permute-start | bytes 49160 | tf_op jit(solution)/shard_map/ppermute | solution.py:16
  147.5 4.5 %collective-permute-start.24 = (f32[2,16,1,128]{3,1,2,0:T(8,128)S(1)}, f32[2,16,1,128]{3,1,2,0:T(8,128)S(1)}, u32[]{:S(2)}, u32[]{:S(2)}) collective-permute-start(f32[2,16,1,128]{3,1,2,0:T(8,128)S(1)} %bitcast.586), channel_id=1, source_target_pairs={{1,0},{3,2},{5,4},{7,6},{9,8},{11,10},{13,12},{15,14},{17,16},{19,... | collective-permute-start | bytes 49160 | tf_op jit(solution)/shard_map/ppermute | solution.py:16
  155.1 5.7 %collective-permute-start.26 = (f32[2,16,1,128]{3,1,2,0:T(8,128)S(1)}, f32[2,16,1,128]{3,1,2,0:T(8,128)S(1)}, u32[]{:S(2)}, u32[]{:S(2)}) collective-permute-start(f32[2,16,1,128]{3,1,2,0:T(8,128)S(1)} %bitcast.593), channel_id=1, source_target_pairs={{0,1},{2,3},{4,5},{6,7},{8,9},{10,11},{12,13},{14,15},{16,17},{18,... | collective-permute-start | bytes 49160 | tf_op jit(solution)/shard_map/ppermute | solution.py:16
  176.5 5.7 %collective-permute-start.30 = (f32[2,16,1,128]{3,1,2,0:T(8,128)S(1)}, f32[2,16,1,128]{3,1,2,0:T(8,128)S(1)}, u32[]{:S(2)}, u32[]{:S(2)}) collective-permute-start(f32[2,16,1,128]{3,1,2,0:T(8,128)S(1)} %bitcast.594), channel_id=1, source_target_pairs={{0,1},{2,3},{4,5},{6,7},{8,9},{10,11},{12,13},{14,15},{16,17},{18,... | collective-permute-start | bytes 49160 | tf_op jit(solution)/shard_map/ppermute | solution.py:16
  (91 other events, 144.0 us)
Sparse Core Ops, SparseCore 0:
  186.2 45.0 reduce-scatter.1
where the time goes:
time: 255 us; the launch traced here: 252 us
  starting transfers between devices  74.4 us (29%)
  blocking collectives  56.3 us (22%)
  local copies, waits for them, and re-layouts  54.1 us (21%)
  waiting for transfers between devices  21.5 us (8%)
  between operations  19.4 us (8%)
  other arithmetic  18.6 us (7%)
  matrix products  7.47 us (3%)
    ppermute x32, starting transfers between devices, shifted(): return lax.ppermute(x, axis, pairs)  74.4 us
    psum x1, blocking collectives, on_device(): misfit = lax.psum(local_misfit, ('tx', 'gx', 'gy'))  56.3 us
    ppermute x32, waiting for transfers between devices, shifted(): return lax.ppermute(x, axis, pairs)  21.5 us
    unnamed x167, local copies, waits for them, and re-layouts  21.2 us
    scatter-add x4, local copies, waits for them, and re-layouts, on_device(): adj_e.at[0:2, :, :, ZREC]  14.4 us
    another operation x6, other arithmetic  10.1 us
    dot_general x4, matrix products, on_device(): jnp.dot(planes, onehot.T, precision=highest) - observe[step_idx]  6.12 us
  transfers between devices with their start and end apart: 33, of which 19 were waited for; matrix products, arithmetic and copies ran while one was open for 5% of the time, Pallas kernels for 0%

commit v1 on v0

v1 whole, which is shorter than its diff:
```python
import functools

import jax
import jax.numpy as jnp
from jax import lax
from jax.experimental import pallas as pl
from jax.experimental.pallas import tpu as pltpu
from jax.sharding import PartitionSpec as P

STEPS = 4
ZREC = 32
STEP_DT = 0.5
HALO = STEPS
LOW = HALO + 1
CHUNK = 4
MESH = pl.DeviceIdType.MESH
DIRS = [(dx, dy) for dx in (-1, 0, 1) for dy in (-1, 0, 1) if (dx, dy) != (0, 0)]


def window_rows(gx_size, size_x):
    return size_x + (HALO if gx_size == 2 else 2 * HALO)


def kernel(
    sizes,
    cond_h, cond_v, fwd, adj, observed, footprint, owner, rec_cells,
    out, misfit_out,
    fw, aw, cw, decay, drive, kept, grad, inj_own, inj_in, inj_win, obs_scr,
    mis_own, mis_in, give, keep, got, part,
    loc_sem, halo_send, halo_recv, inj_send, inj_recv, mis_send, mis_recv,
    sib_send, sib_recv, z_send, z_recv,
):
    n_tx, n_gx, n_gy = sizes
    nz = n_tx // 2
    size_x, size_y, depth = cond_h.shape
    rows_w = window_rows(n_gx, size_x)
    wy = size_y + 2 * HALO
    it, ix, iy = lax.axis_index("tx"), lax.axis_index("gx"), lax.axis_index("gy")
    core = lax.rem(it, 2)
    iz = it // 2
    has = {}
    for dx, dy in DIRS:
        ok = None
        for d, i, n in ((dx, ix, n_gx), (dy, iy, n_gy)):
            if d:
                one = (i > 0) if d < 0 else (i < n - 1)
                ok = one if ok is None else jnp.logical_and(ok, one)
        has[(dx, dy)] = ok
    has_lo, has_hi = has[(-1, 0)], has[(1, 0)]
    start = jnp.where(has_lo, -HALO, 0)

    def plane_partner(k):
        ox, oy = k // n_gy, k % n_gy
        return {"gx": lax.rem(ix + ox, n_gx), "gy": lax.rem(iy + oy, n_gy)}

    sibling = {"tx": it + 1 - 2 * core}

    def z_partner(dz):
        return lax.rem(iz + dz, nz)

    tile_x, tile_y = pl.ds(LOW, size_x), pl.ds(0, size_y)
    locals_ = [
        pltpu.make_async_copy(cond_h, cw.at[0, tile_x, tile_y], loc_sem.at[0]),
        pltpu.make_async_copy(cond_v, cw.at[1, tile_x, tile_y], loc_sem.at[1]),
        pltpu.make_async_copy(fwd.at[0], fw.at[:, tile_x, tile_y], loc_sem.at[2]),
        pltpu.make_async_copy(adj.at[0], aw.at[:, tile_x, tile_y], loc_sem.at[3]),
    ]
    for c in locals_:
        c.start()

    rows_all = fw.shape[1]
    for ref in (cw, fw, aw):
        comps = ref.shape[0]
        ref[:, 0:LOW] = jnp.zeros((comps, LOW, wy, depth), jnp.float32)
        top = LOW + size_x
        ref[:, top:rows_all] = jnp.zeros((comps, rows_all - top, wy, depth), jnp.float32)
        ref[:, LOW:top, size_y:wy] = jnp.zeros((comps, size_x, wy - size_y, depth), jnp.float32)
    inj_in[...] = jnp.zeros_like(inj_in)

    barrier = pltpu.get_barrier_semaphore()
    for k in range(1, n_gx * n_gy):
        pl.semaphore_signal(barrier, inc=1, device_id=plane_partner(k), device_id_type=MESH)
    pl.semaphore_signal(barrier, inc=1, device_id=sibling, device_id_type=MESH)
    for dz in range(1, nz):
        pl.semaphore_signal(
            barrier, inc=1, device_id={"tx": 2 * z_partner(dz) + core}, device_id_type=MESH
        )
    pl.semaphore_wait(barrier, n_gx * n_gy - 1 + 1 + nz - 1)

    def source(d, size):
        return pl.ds(0, size) if d == 0 else (pl.ds(size - HALO, HALO) if d > 0 else pl.ds(0, HALO))

    def target_x(d):
        return tile_x if d == 0 else (pl.ds(LOW - HALO, HALO) if d > 0 else pl.ds(LOW + size_x, HALO))

    def target_y(d):
        return tile_y if d == 0 else (pl.ds(size_y + HALO, HALO) if d > 0 else pl.ds(size_y, HALO))

    def halo_copy(which, d):
        dx, dy = DIRS[d]
        sx, sy = source(dx, size_x), source(dy, size_y)
        tx_, ty_ = target_x(dx), target_y(dy)
        src, dst = {
            0: (cond_h.at[sx, sy], cw.at[0, tx_, ty_]),
            1: (cond_v.at[sx, sy], cw.at[1, tx_, ty_]),
            2: (fwd.at[0, :, sx, sy], fw.at[:, tx_, ty_]),
            3: (adj.at[0, :, sx, sy], aw.at[:, tx_, ty_]),
        }[which]
        return pltpu.make_async_remote_copy(
            src_ref=src, dst_ref=dst,
            send_sem=halo_send.at[which, d], recv_sem=halo_recv.at[which, d],
            device_id={"gx": ix + dx, "gy": iy + dy}, device_id_type=MESH,
        )

    def each_dir(fn, conds):
        for d, (dx, dy) in enumerate(DIRS):
            if (dx and n_gx == 1) or (dy and n_gy == 1):
                continue
            pl.when(conds(dx, dy))(functools.partial(fn, d))

    def to_side(dx, dy):
        return has[(dx, dy)]

    def from_side(dx, dy):
        return has[(-dx, -dy)]

    for which in range(4):
        each_dir(lambda d, w=which: halo_copy(w, d).start(), to_side)

    lanes = lax.broadcasted_iota(jnp.int32, (size_y, depth), 1)
    highest = lax.Precision.HIGHEST
    rpt = rec_cells.shape[-1]
    cells = rec_cells[0]
    in_y = (lax.broadcasted_iota(jnp.int32, (size_y, rpt), 0) == cells % size_y).astype(jnp.float32)
    in_x = (lax.broadcasted_iota(jnp.int32, (size_x, rpt), 0) == cells // size_y).astype(jnp.float32)
    lane_x = (
        lax.broadcasted_iota(jnp.int32, (size_x, depth), 0)
        == lax.broadcasted_iota(jnp.int32, (size_x, depth), 1) % size_x
    ).astype(jnp.float32)
    lane_k = (
        lax.broadcasted_iota(jnp.int32, (2 * STEPS, depth), 0)
        == lax.broadcasted_iota(jnp.int32, (2 * STEPS, depth), 1) // size_x
    ).astype(jnp.float32)
    for n in range(STEPS):
        obs_scr[2 * n : 2 * n + 2, 0:rpt] = observed[0, n, 0, 0]
    over0 = (((0,), (0,)), ((), ()))
    at_x = lax.dot_general(in_x, lane_x, over0, precision=highest, preferred_element_type=jnp.float32)
    obs_l = at_x * lax.dot_general(
        obs_scr[:, 0:rpt], lane_k, over0, precision=highest, preferred_element_type=jnp.float32
    )
    count = jnp.dot(in_y, at_x, precision=highest, preferred_element_type=jnp.float32)
    obs_sum = jnp.dot(in_y, obs_l, precision=highest, preferred_element_type=jnp.float32)

    for n in range(STEPS):
        for x in sorted({size_x, size_x + HALO, rows_w}):
            kept[n, :, LOW + x] = jnp.zeros((3, wy, depth), jnp.float32)

    def wait_in(which):
        locals_[which].wait()
        each_dir(lambda d: halo_copy(which, d).wait_recv(), from_side)

    wait_in(0)
    wait_in(1)
    sub = lax.broadcasted_iota(jnp.int32, (wy, depth), 0)
    lane = lax.broadcasted_iota(jnp.int32, (wy, depth), 1)
    y_hi = jnp.where(has[(0, 1)], 1.0, 0.0)
    y_lo = jnp.where(has[(0, -1)], 1.0, 0.0)
    y_ok = jnp.where(sub < size_y, 1.0, jnp.where(sub < size_y + HALO, y_hi, y_lo))
    half = STEP_DT * y_ok
    chunks = rows_w // CHUNK

    def coefficients(k, carry):
        for i in range(CHUNK):
            x = start + k * CHUNK + i
            ok = y_ok * jnp.where(jnp.logical_or(x < size_x, has_hi), 1.0, 0.0)
            for c in range(2):
                rate = 0.25 * cw[c, x + LOW]
                scaled = ok / (1.0 + rate)
                drive[c, x + LOW] = STEP_DT * scaled
                decay[c, x + LOW] = (1.0 - rate) * scaled
        return carry

    lax.fori_loop(0, chunks, coefficients, 0)

    def y_next(f):
        return pltpu.roll(f, wy - 1, 0)

    def y_prev(f):
        return pltpu.roll(f, 1, 0)

    def z_next(f):
        return jnp.where(lane == depth - 1, 0.0, pltpu.roll(f, depth - 1, 1))

    def z_prev(f):
        return jnp.where(lane == 0, 0.0, pltpu.roll(f, 1, 1))

    def step_rows(r, e_src, h, e_dst, after):
        e = [[e_src[c, r + i] for c in range(3)] for i in range(CHUNK)]
        last = r + CHUNK
        e.append([None, e_src[1, last], e_src[2, last]])
        hp_y, hp_z = h[1, r - 1], h[2, r - 1]
        for i in range(CHUNK):
            ex, ey, ez = e[i]
            _, ey_n, ez_n = e[i + 1]
            hx = h[0, r + i] - half * ((y_next(ez) - ez) - (z_next(ey) - ey))
            hy = h[1, r + i] - half * ((z_next(ex) - ex) - (ez_n - ez))
            hz = h[2, r + i] - half * ((ey_n - ey) - (y_next(ex) - ex))
            h[0, r + i] = hx
            h[1, r + i] = hy
            h[2, r + i] = hz
            cx = (hz - y_prev(hz)) - (hy - z_prev(hy))
            cy = (hx - z_prev(hx)) - (hz - hp_z)
            cz = (hy - hp_y) - (hx - y_prev(hx))
            hp_y, hp_z = hy, hz
            dec_h, drv_h = decay[0, r + i], drive[0, r + i]
            dec_v, drv_v = decay[1, r + i], drive[1, r + i]
            new = (dec_h * ex + drv_h * cx, dec_h * ey + drv_h * cy, dec_v * ez + drv_v * cz)
            for c in range(3):
                e_dst[c, r + i] = new[c]
            if after is not None:
                after(r + i, new)

    def step(e_src, h, e_dst, after=None):
        def body(k, carry):
            step_rows(start + LOW + k * CHUNK, e_src, h, e_dst, after)
            return carry

        lax.fori_loop(0, chunks, body, 0)

    wait_in(2)
    for n in range(STEPS):
        step(fw.at[0:3] if n == 0 else kept.at[n - 1], fw.at[3:6], kept.at[n])

    rec = jnp.zeros((size_y, depth), jnp.float32)
    for n in range(STEPS):
        for c in range(2):
            for x in range(size_x):
                at = (2 * n + c) * size_x + x
                e = kept[n, c, LOW + x, 0:size_y]
                rec = jnp.where(lanes == at, pltpu.roll(e, (at - ZREC) % depth, 1), rec)
    inj_own[...] = count * rec - obs_sum

    def inj_copy(d):
        dx, dy = DIRS[d]
        return pltpu.make_async_remote_copy(
            src_ref=inj_own, dst_ref=inj_in.at[(1 - dx) * 3 + 1 - dy],
            send_sem=inj_send.at[d], recv_sem=inj_recv.at[d],
            device_id={"gx": ix + dx, "gy": iy + dy}, device_id_type=MESH,
        )

    each_dir(lambda d: inj_copy(d).start(), to_side)

    at_rec = lax.dot_general(in_y, rec, over0, precision=highest, preferred_element_type=jnp.float32)
    resid = at_x * at_rec - obs_l
    mis_own[...] = 0.5 * jnp.sum((resid * resid).reshape(rpt // 8, 8, depth), axis=0)

    def mis_copy(k):
        return pltpu.make_async_remote_copy(
            src_ref=mis_own, dst_ref=mis_in.at[k],
            send_sem=mis_send.at[k], recv_sem=mis_recv.at[k],
            device_id=plane_partner(k), device_id_type=MESH,
        )

    for k in range(1, n_gx * n_gy):
        mis_copy(k).start()

    wait_in(3)
    each_dir(lambda d: inj_copy(d).wait_recv(), from_side)
    sub8 = lax.broadcasted_iota(jnp.int32, (2 * HALO, depth), 0)
    for q in range(3):
        own = inj_own[...] if q == 1 else inj_in[q * 3 + 1]
        inj_win[q, 0:size_y] = own
        inj_win[q, size_y:wy] = jnp.where(
            sub8 < HALO,
            inj_in[q * 3 + 2, 0 : 2 * HALO],
            inj_in[q * 3, size_y - 2 * HALO : size_y],
        )

    for n in reversed(range(STEPS)):

        def inject(k, carry, n=n):
            for i in range(CHUNK):
                x = start + k * CHUNK + i
                plane = inj_win[(x + size_x) // size_x]
                for c in range(2):
                    at = (2 * n + c) * size_x + lax.rem(x + size_x, size_x)
                    moved = pltpu.roll(plane, lax.rem(ZREC + depth - at, depth), 1)
                    aw[c, x + LOW] = aw[c, x + LOW] + jnp.where(lane == ZREC, moved, 0.0)
            return carry

        lax.fori_loop(0, chunks, inject, 0)

        def add_gradient(r, new, n=n):
            tile = slice(0, size_y)
            g_h = new[0][tile] * kept[n, 0, r, tile] + new[1][tile] * kept[n, 1, r, tile]
            g_v = new[2][tile] * kept[n, 2, r, tile]
            if n < STEPS - 1:
                g_h = grad[0, r] + g_h
                g_v = grad[1, r] + g_v
            grad[0, r] = g_h
            grad[1, r] = g_v

        step(aw.at[0:3], aw.at[3:6], aw.at[0:3], add_gradient)

    for k in range(1, n_gx * n_gy):
        mis_copy(k).wait_recv()
    misfit = mis_own[...]
    for k in range(1, n_gx * n_gy):
        misfit = misfit + mis_in[k]

    flag = footprint[0, 0, 0].astype(jnp.float32)
    block = size_x // n_tx
    cells_rows = 2 * block * size_y

    def ordered(dst, dz, to_core):
        z = z_partner(dz)
        first = owner[0, 0, 2 * z + to_core] * block
        for c in range(2):
            for b in range(block):
                at = (c * block + b) * size_y
                dst[dz, at : at + size_y] = flag * grad[c, LOW + first + b]
        dst[dz, cells_rows : cells_rows + 8] = misfit

    def sib_copy(dz):
        return pltpu.make_async_remote_copy(
            src_ref=give.at[dz], dst_ref=got.at[dz],
            send_sem=sib_send.at[dz], recv_sem=sib_recv.at[dz],
            device_id=sibling, device_id_type=MESH,
        )

    def z_copy(dz):
        return pltpu.make_async_remote_copy(
            src_ref=keep.at[dz], dst_ref=part.at[dz],
            send_sem=z_send.at[dz], recv_sem=z_recv.at[dz],
            device_id={"tx": 2 * z_partner(dz) + core}, device_id_type=MESH,
        )

    order = list(range(1, nz)) + [0]
    for dz in order:
        ordered(give, dz, 1 - core)
        sib_copy(dz).start()
    for dz in order:
        ordered(keep, dz, core)
    for dz in order:
        sib_copy(dz).wait_recv()
        keep[dz] = keep[dz] + got[dz]
        if dz:
            z_copy(dz).start()
    for dz in range(1, nz):
        z_copy(dz).wait_recv()
    total = keep[0]
    for dz in range(1, nz):
        total = total + part[dz]
    for c in range(2):
        for b in range(block):
            at = (c * block + b) * size_y
            out[0, 0, c, b] = total[at : at + size_y]
    misfit_out[0, 0] = jnp.sum(total[cells_rows : cells_rows + 8])

    for which in range(4):
        each_dir(lambda d, w=which: halo_copy(w, d).wait_send(), to_side)
    each_dir(lambda d: inj_copy(d).wait_send(), to_side)
    for k in range(1, n_gx * n_gy):
        mis_copy(k).wait_send()
    for dz in order:
        sib_copy(dz).wait_send()
    for dz in range(1, nz):
        z_copy(dz).wait_send()


def on_device(sizes, cond_h, cond_v, fwd_init, adj_init, observed, footprint, owner, rec_cells):
    n_tx, n_gx, n_gy = sizes
    nz = n_tx // 2
    size_x, size_y, depth = cond_h.shape
    rows_w = window_rows(n_gx, size_x)
    rows = LOW + rows_w + 1
    wy = size_y + 2 * HALO
    block = size_x // n_tx
    packed = 2 * block * size_y + 8
    f32 = jnp.float32
    n_dirs = len(DIRS)
    plane = n_gx * n_gy
    dma = pltpu.SemaphoreType.DMA
    hbm, vmem, smem = pl.ANY, pltpu.VMEM, pltpu.SMEM
    owned, misfit = pl.pallas_call(
        functools.partial(kernel, sizes),
        out_shape=(
            jax.ShapeDtypeStruct((1, 1, 2, block, size_y, depth), f32),
            jax.ShapeDtypeStruct((1, 1), f32),
        ),
        in_specs=[
            pl.BlockSpec(memory_space=s) for s in (hbm, hbm, hbm, hbm, vmem, smem, smem, vmem)
        ],
        out_specs=(pl.BlockSpec(memory_space=vmem), pl.BlockSpec(memory_space=smem)),
        scratch_shapes=[
            vmem((6, rows, wy, depth), f32),
            vmem((6, rows, wy, depth), f32),
            vmem((2, rows, wy, depth), f32),
            vmem((2, rows, wy, depth), f32),
            vmem((2, rows, wy, depth), f32),
            vmem((STEPS, 3, rows, wy, depth), f32),
            vmem((2, rows, size_y, depth), f32),
            vmem((size_y, depth), f32),
            vmem((9, size_y, depth), f32),
            vmem((3, wy, depth), f32),
            vmem((2 * STEPS, depth), f32),
            vmem((8, depth), f32),
            vmem((plane, 8, depth), f32),
            vmem((nz, packed, depth), f32),
            vmem((nz, packed, depth), f32),
            vmem((nz, packed, depth), f32),
            vmem((nz, packed, depth), f32),
            dma((4,)),
            dma((4, n_dirs)),
            dma((4, n_dirs)),
            dma((n_dirs,)),
            dma((n_dirs,)),
            dma((plane,)),
            dma((plane,)),
            dma((nz,)),
            dma((nz,)),
            dma((nz,)),
            dma((nz,)),
        ],
        compiler_params=pltpu.CompilerParams(
            collective_id=0, has_side_effects=True, vmem_limit_bytes=40 * 1024 * 1024
        ),
    )(cond_h, cond_v, fwd_init, adj_init, observed, footprint, owner, rec_cells)
    return owned, misfit.reshape(())


def solution(mesh):
    placed = (
        P("gx", "gy", None),
        P("gx", "gy", None),
        P("tx", None, "gx", "gy", None),
        P("tx", None, "gx", "gy", None),
        P("tx", None, "gx", "gy", None, None),
        P("tx", "gx", "gy"),
        P("gx", "gy", None),
        P("gx", "gy", None),
    )
    sizes = (mesh.shape["tx"], mesh.shape["gx"], mesh.shape["gy"])
    return jax.shard_map(
        functools.partial(on_device, sizes),
        mesh=mesh,
        in_specs=placed,
        out_specs=(P("gx", "tx", None, None, "gy", None), P()),
        check_vma=False,
    )
```

time: 255 us -> 43.9 us (0.17); the launches traced: 252 us -> 43.6 us
  starting transfers between devices: 74.4 us -> 0 us
  blocking collectives: 56.3 us -> 0 us
  local copies, waits for them, and re-layouts: 54.1 us -> 5.38 us
  Pallas kernels: 0 us -> 35.2 us
  waiting for transfers between devices: 21.5 us -> 0 us
  other arithmetic: 18.6 us -> 0 us
  between operations: 19.4 us -> 3.04 us
  matrix products: 7.47 us -> 0 us
    ppermute x32 -> x0, starting transfers between devices: 74.4 us -> none  [shifted(): return lax.ppermute(x, axis, pairs)]
    psum x1 -> x0, blocking collectives: 56.3 us -> none  [on_device(): misfit = lax.psum(local_misfit, ('tx', 'gx', 'gy'))]
    pallas_call x0 -> x1, Pallas kernels: none -> 35.2 us  [on_device(): pl.pallas_call(functools.partial(kernel, sizes), out_shape=(jax.ShapeDtyp...]
    ppermute x32 -> x0, waiting for transfers between devices: 21.5 us -> none  [shifted(): return lax.ppermute(x, axis, pairs)]
    unnamed x167 -> x15, local copies, waits for them, and re-layouts: 21.2 us -> 5.38 us
    scatter-add x4 -> x0, local copies, waits for them, and re-layouts: 14.4 us -> none  [on_device(): adj_e.at[0:2, :, :, ZREC]]
    another operation x23 -> x0, other arithmetic: 12.1 us -> none
    slice x88 -> x0, local copies, waits for them, and re-layouts: 9.05 us -> none  [the longest x32 4.39 us: ahead_of(): lax.slice_in_dim(values, 1, extent, axis=axis_num)]
  transfers between devices with their start and end apart: 33 -> 0, of which waited for: 19 -> 0; matrix products, arithmetic and copies ran while one was open for 5% -> 0% of each run, Pallas kernels for 0% -> 0%
where the time goes in v1:
time: 43.9 us; the launch traced here: 43.6 us
  Pallas kernels  35.2 us (80%)
  local copies, waits for them, and re-layouts  5.38 us (12%)
  between operations  3.04 us (7%)
    pallas_call x1, Pallas kernels, on_device(): pl.pallas_call(functools.partial(kernel, sizes), out_shape=(jax.ShapeDtyp...  35.2 us
    unnamed x15, local copies, waits for them, and re-layouts  5.38 us

profile of v1, /device:TPU:1, one launch (start us, length us, event | category | flops | bytes accessed | tf_op | source)
XLA Modules:
  0.0 43.6 jit_solution(4857917120628007919)
XLA Ops:
  0.6 0.0 copy-start.6
  0.6 0.0 copy-start.5
  1.3 0.0 copy-done.6
  1.3 0.0 copy-done.5
  1.3 0.0 copy-start
  1.3 1.1 %copy-done = f32[1,6,16,16,128]{4,3,2,1,0:T(8,128)S(1)} copy-done((f32[1,6,16,16,128]{4,3,2,1,0:T(8,128)S(1)}, f32[1,6,16,16,128]{4,3,2,1,0:T(8,128)}, u32[]{:S(2)}) %copy-start) | copy-done | bytes 786456
  2.5 0.0 copy-start.1
  2.5 1.1 %copy-done.1 = f32[1,6,16,16,128]{4,3,2,1,0:T(8,128)S(1)} copy-done((f32[1,6,16,16,128]{4,3,2,1,0:T(8,128)S(1)}, f32[1,6,16,16,128]{4,3,2,1,0:T(8,128)}, u32[]{:S(2)}) %copy-start.1) | copy-done | bytes 786456
  3.6 0.0 copy-start.2
  3.6 0.9 %copy-done.2 = f32[16,16,128]{2,1,0:T(8,128)S(1)} copy-done((f32[16,16,128]{2,1,0:T(8,128)S(1)}, f32[16,16,128]{2,1,0:T(8,128)}, u32[]{:S(2)}) %copy-start.2) | copy-done | bytes 131096
  4.5 0.0 copy-start.3
  4.5 0.9 %copy-done.3 = f32[16,16,128]{2,1,0:T(8,128)S(1)} copy-done((f32[16,16,128]{2,1,0:T(8,128)S(1)}, f32[16,16,128]{2,1,0:T(8,128)}, u32[]{:S(2)}) %copy-start.3) | copy-done | bytes 131096
  5.4 0.0 copy-start.4
  5.4 0.7 %copy-done.4 = f32[1,4,1,1,2,32]{5,4,3,2,1,0:T(2,128)S(1)} copy-done((f32[1,4,1,1,2,32]{5,4,3,2,1,0:T(2,128)S(1)}, f32[1,4,1,1,2,32]{5,4,3,2,1,0:T(2,128)}, u32[]{:S(2)}) %copy-start.4) | copy-done | bytes 1048
  6.1 35.2 %shard_map.95 = (f32[1,1,2,2,16,128]{5,4,3,2,1,0:T(8,128)S(1)}, f32[1,1]{1,0:T(1,128)}) custom-call(f32[16,16,128]{2,1,0:T(8,128)S(1)} %copy-done.2, f32[16,16,128]{2,1,0:T(8,128)S(1)} %copy-done.3, f32[1,6,16,16,128]{4,3,2,1,0:T(8,128)S(1)} %copy-done, f32[1,6,16,16,128]{4,3,2,1,0:T(8,128)S(1)} %copy-done.1, f32[1,4,1,1,2,32]{5,4,3,2,1,0:T(2,128)S(1)} %copy-done.4, ...), custom_call_target="tpu_custom_call" | custom-call | tf_op jit(solution)/shard_map/pallas_call | solution.py:385
  41.3 0.6 %copy.13 = f32[1,1,2,2,16,128]{5,4,3,2,1,0:T(8,128)} copy(f32[1,1,2,2,16,128]{5,4,3,2,1,0:T(8,128)S(1)} %get-tuple-element.8) | data formatting | bytes 65536
Async XLA Ops:
  0.6 0.7 %copy-start.6 = (s32[1,1,32]{2,1,0:T(1,128)S(1)}, s32[1,1,32]{2,1,0:T(1,128)}, u32[]{:S(2)}) copy-start(s32[1,1,32]{2,1,0:T(1,128)} %rec_cells.1) | copy-start | bytes 388
  0.6 0.7 %copy-start.5 = (s32[1,1,8]{2,1,0:T(1,128)S(1)}, s32[1,1,8]{2,1,0:T(1,128)}, u32[]{:S(2)}) copy-start(s32[1,1,8]{2,1,0:T(1,128)} %owner.1) | copy-start | bytes 100
  1.3 1.1 %copy-start = (f32[1,6,16,16,128]{4,3,2,1,0:T(8,128)S(1)}, f32[1,6,16,16,128]{4,3,2,1,0:T(8,128)}, u32[]{:S(2)}) copy-start(f32[1,6,16,16,128]{4,3,2,1,0:T(8,128)} %fwd.1) | copy-start | bytes 2359300
  2.5 1.1 %copy-start.1 = (f32[1,6,16,16,128]{4,3,2,1,0:T(8,128)S(1)}, f32[1,6,16,16,128]{4,3,2,1,0:T(8,128)}, u32[]{:S(2)}) copy-start(f32[1,6,16,16,128]{4,3,2,1,0:T(8,128)} %adj.1) | copy-start | bytes 2359300
  3.6 0.9 %copy-start.2 = (f32[16,16,128]{2,1,0:T(8,128)S(1)}, f32[16,16,128]{2,1,0:T(8,128)}, u32[]{:S(2)}) copy-start(f32[16,16,128]{2,1,0:T(8,128)} %cond_h.1) | copy-start | bytes 393220
  4.5 0.9 %copy-start.3 = (f32[16,16,128]{2,1,0:T(8,128)S(1)}, f32[16,16,128]{2,1,0:T(8,128)}, u32[]{:S(2)}) copy-start(f32[16,16,128]{2,1,0:T(8,128)} %cond_v.1) | copy-start | bytes 393220
  5.4 0.7 %copy-start.4 = (f32[1,4,1,1,2,32]{5,4,3,2,1,0:T(2,128)S(1)}, f32[1,4,1,1,2,32]{5,4,3,2,1,0:T(2,128)}, u32[]{:S(2)}) copy-start(f32[1,4,1,1,2,32]{5,4,3,2,1,0:T(2,128)} %observed.1) | copy-start | bytes 3076

commit v2 on v1

--- a/solution.py
+++ b/solution.py
@@ -12,7 +12,6 @@
 STEP_DT = 0.5
 HALO = STEPS
 LOW = HALO + 1
-CHUNK = 4
 MESH = pl.DeviceIdType.MESH
 DIRS = [(dx, dy) for dx in (-1, 0, 1) for dy in (-1, 0, 1) if (dx, dy) != (0, 0)]
 
@@ -23,9 +22,10 @@
 
 def kernel(
     sizes,
-    cond_h, cond_v, fwd, adj, observed, footprint, owner, rec_cells,
+    cond_h, cond_v, fwd, adj, observed_in, footprint_in, owner_in, rec_in,
     out, misfit_out,
     fw, aw, cw, decay, drive, kept, grad, inj_own, inj_in, inj_win, obs_scr,
+    observed, footprint, owner, rec_cells,
     mis_own, mis_in, give, keep, got, part,
     loc_sem, halo_send, halo_recv, inj_send, inj_recv, mis_send, mis_recv,
     sib_send, sib_recv, z_send, z_recv,
@@ -64,17 +64,24 @@
         pltpu.make_async_copy(cond_v, cw.at[1, tile_x, tile_y], loc_sem.at[1]),
         pltpu.make_async_copy(fwd.at[0], fw.at[:, tile_x, tile_y], loc_sem.at[2]),
         pltpu.make_async_copy(adj.at[0], aw.at[:, tile_x, tile_y], loc_sem.at[3]),
+        pltpu.make_async_copy(observed_in, observed, loc_sem.at[4]),
+        pltpu.make_async_copy(rec_in, rec_cells, loc_sem.at[5]),
+        pltpu.make_async_copy(footprint_in, footprint, loc_sem.at[6]),
+        pltpu.make_async_copy(owner_in, owner, loc_sem.at[7]),
     ]
     for c in locals_:
         c.start()
 
     rows_all = fw.shape[1]
+    top = LOW + size_x
     for ref in (cw, fw, aw):
         comps = ref.shape[0]
-        ref[:, 0:LOW] = jnp.zeros((comps, LOW, wy, depth), jnp.float32)
-        top = LOW + size_x
-        ref[:, top:rows_all] = jnp.zeros((comps, rows_all - top, wy, depth), jnp.float32)
-        ref[:, LOW:top, size_y:wy] = jnp.zeros((comps, size_x, wy - size_y, depth), jnp.float32)
+        ref[:, :, size_y:wy] = jnp.zeros((comps, rows_all, wy - size_y, depth), jnp.float32)
+        if ref is cw and n_gx == 2:
+            continue
+        zero_rows = (LOW - 1, top) if n_gx == 2 else (*range(LOW), *range(top, rows_all))
+        for r in zero_rows:
+            ref[:, r, 0:size_y] = jnp.zeros((comps, size_y, depth), jnp.float32)
     inj_in[...] = jnp.zeros_like(inj_in)
 
     barrier = pltpu.get_barrier_semaphore()
@@ -87,11 +94,11 @@
         )
     pl.semaphore_wait(barrier, n_gx * n_gy - 1 + 1 + nz - 1)
 
-    def source(d, size):
-        return pl.ds(0, size) if d == 0 else (pl.ds(size - HALO, HALO) if d > 0 else pl.ds(0, HALO))
-
-    def target_x(d):
-        return tile_x if d == 0 else (pl.ds(LOW - HALO, HALO) if d > 0 else pl.ds(LOW + size_x, HALO))
+    def source(d, size, deep=HALO):
+        return pl.ds(0, size) if d == 0 else (pl.ds(size - deep, deep) if d > 0 else pl.ds(0, deep))
+
+    def target_x(d, deep=HALO):
+        return tile_x if d == 0 else (pl.ds(LOW - deep, deep) if d > 0 else pl.ds(LOW + size_x, deep))
 
     def target_y(d):
         return tile_y if d == 0 else (pl.ds(size_y + HALO, HALO) if d > 0 else pl.ds(size_y, HALO))
@@ -100,6 +107,8 @@
         dx, dy = DIRS[d]
         sx, sy = source(dx, size_x), source(dy, size_y)
         tx_, ty_ = target_x(dx), target_y(dy)
+        if which < 2:
+            sx, tx_ = source(dx, size_x, HALO - 1), target_x(dx, HALO - 1)
         src, dst = {
             0: (cond_h.at[sx, sy], cw.at[0, tx_, ty_]),
             1: (cond_v.at[sx, sy], cw.at[1, tx_, ty_]),
@@ -124,10 +133,12 @@
     def from_side(dx, dy):
         return has[(-dx, -dy)]
 
-    for which in range(4):
+    for which in range(3):
         each_dir(lambda d, w=which: halo_copy(w, d).start(), to_side)
 
     lanes = lax.broadcasted_iota(jnp.int32, (size_y, depth), 1)
+    for c in locals_[4:]:
+        c.wait()
     highest = lax.Precision.HIGHEST
     rpt = rec_cells.shape[-1]
     cells = rec_cells[0]
@@ -167,11 +178,17 @@
     y_lo = jnp.where(has[(0, -1)], 1.0, 0.0)
     y_ok = jnp.where(sub < size_y, 1.0, jnp.where(sub < size_y + HALO, y_hi, y_lo))
     half = STEP_DT * y_ok
-    chunks = rows_w // CHUNK
+
+    def span(j):
+        if n_gx == 2:
+            rows = rows_w - j + j % 2
+            return jnp.where(has_lo, j - HALO, 0), rows // 2, 2
+        return start, 8, rows_w // 8
+
 
     def coefficients(k, carry):
-        for i in range(CHUNK):
-            x = start + k * CHUNK + i
+        for i in range(rows_w // 4):
+            x = start + k * (rows_w // 4) + i
             ok = y_ok * jnp.where(jnp.logical_or(x < size_x, has_hi), 1.0, 0.0)
             for c in range(2):
                 rate = 0.25 * cw[c, x + LOW]
@@ -180,7 +197,7 @@
                 decay[c, x + LOW] = (1.0 - rate) * scaled
         return carry
 
-    lax.fori_loop(0, chunks, coefficients, 0)
+    lax.fori_loop(0, 4, coefficients, 0)
 
     def y_next(f):
         return pltpu.roll(f, wy - 1, 0)
@@ -194,14 +211,12 @@
     def z_prev(f):
         return jnp.where(lane == 0, 0.0, pltpu.roll(f, 1, 1))
 
-    def step_rows(r, e_src, h, e_dst, after):
-        e = [[e_src[c, r + i] for c in range(3)] for i in range(CHUNK)]
-        last = r + CHUNK
-        e.append([None, e_src[1, last], e_src[2, last]])
+    def step_rows(r, chunk, e_src, h, e_dst, after):
+        ex, ey, ez = (e_src[c, r] for c in range(3))
         hp_y, hp_z = h[1, r - 1], h[2, r - 1]
-        for i in range(CHUNK):
-            ex, ey, ez = e[i]
-            _, ey_n, ez_n = e[i + 1]
+        for i in range(chunk):
+            ey_n, ez_n = e_src[1, r + i + 1], e_src[2, r + i + 1]
+            ex_n = e_src[0, r + i + 1] if i < chunk - 1 else None
             hx = h[0, r + i] - half * ((y_next(ez) - ez) - (z_next(ey) - ey))
             hy = h[1, r + i] - half * ((z_next(ex) - ex) - (ez_n - ez))
             hz = h[2, r + i] - half * ((ey_n - ey) - (y_next(ex) - ex))
@@ -219,17 +234,21 @@
                 e_dst[c, r + i] = new[c]
             if after is not None:
                 after(r + i, new)
-
-    def step(e_src, h, e_dst, after=None):
+            ex, ey, ez = ex_n, ey_n, ez_n
+
+    def step(j, e_src, h, e_dst, after=None):
+        first, chunk, chunks = span(j)
+
         def body(k, carry):
-            step_rows(start + LOW + k * CHUNK, e_src, h, e_dst, after)
+            step_rows(first + LOW + k * chunk, chunk, e_src, h, e_dst, after)
             return carry
 
         lax.fori_loop(0, chunks, body, 0)
 
     wait_in(2)
+    each_dir(lambda d: halo_copy(3, d).start(), to_side)
     for n in range(STEPS):
-        step(fw.at[0:3] if n == 0 else kept.at[n - 1], fw.at[3:6], kept.at[n])
+        step(n, fw.at[0:3] if n == 0 else kept.at[n - 1], fw.at[3:6], kept.at[n])
 
     rec = jnp.zeros((size_y, depth), jnp.float32)
     for n in range(STEPS):
@@ -277,10 +296,11 @@
         )
 
     for n in reversed(range(STEPS)):
-
-        def inject(k, carry, n=n):
-            for i in range(CHUNK):
-                x = start + k * CHUNK + i
+        first, chunk, chunks = span(STEPS - 1 - n)
+
+        def inject(k, carry, n=n, first=first, chunk=chunk):
+            for i in range(chunk):
+                x = first + k * chunk + i
                 plane = inj_win[(x + size_x) // size_x]
                 for c in range(2):
                     at = (2 * n + c) * size_x + lax.rem(x + size_x, size_x)
@@ -300,7 +320,7 @@
             grad[0, r] = g_h
             grad[1, r] = g_v
 
-        step(aw.at[0:3], aw.at[3:6], aw.at[0:3], add_gradient)
+        step(STEPS - 1 - n, aw.at[0:3], aw.at[3:6], aw.at[0:3], add_gradient)
 
     for k in range(1, n_gx * n_gy):
         mis_copy(k).wait_recv()
@@ -389,7 +409,7 @@
             jax.ShapeDtypeStruct((1, 1), f32),
         ),
         in_specs=[
-            pl.BlockSpec(memory_space=s) for s in (hbm, hbm, hbm, hbm, vmem, smem, smem, vmem)
+            pl.BlockSpec(memory_space=s) for s in [hbm] * 8
         ],
         out_specs=(pl.BlockSpec(memory_space=vmem), pl.BlockSpec(memory_space=smem)),
         scratch_shapes=[
@@ -404,13 +424,17 @@
             vmem((9, size_y, depth), f32),
             vmem((3, wy, depth), f32),
             vmem((2 * STEPS, depth), f32),
+            vmem(observed.shape, f32),
+            smem(footprint.shape, jnp.int32),
+            smem(owner.shape, jnp.int32),
+            vmem(rec_cells.shape, jnp.int32),
             vmem((8, depth), f32),
             vmem((plane, 8, depth), f32),
             vmem((nz, packed, depth), f32),
             vmem((nz, packed, depth), f32),
             vmem((nz, packed, depth), f32),
             vmem((nz, packed, depth), f32),
-            dma((4,)),
+            dma((8,)),
             dma((4, n_dirs)),
             dma((4, n_dirs)),
             dma((n_dirs,)),
@@ -423,7 +447,7 @@
             dma((nz,)),
         ],
         compiler_params=pltpu.CompilerParams(
-            collective_id=0, has_side_effects=True, vmem_limit_bytes=40 * 1024 * 1024
+            collective_id=0, has_side_effects=True, vmem_limit_bytes=60 * 1024 * 1024
         ),
     )(cond_h, cond_v, fwd_init, adj_init, observed, footprint, owner, rec_cells)
     return owned, misfit.reshape(())

time: 43.9 us -> 36 us (0.82)
  local copies, waits for them, and re-layouts: 5.38 us -> 1.38 us
  Pallas kernels: 35.2 us -> 31.4 us
    unnamed x15 -> x1, local copies, waits for them, and re-layouts: 5.38 us -> 1.38 us
    pallas_call x1, Pallas kernels: 35.2 us -> 31.4 us  [on_device(): pl.pallas_call(functools.partial(kernel, sizes), out_shape=(jax.ShapeDtyp...]
where the time goes in v2:
time: 36 us; the launch traced here: 35.8 us
  Pallas kernels  31.4 us (87%)
  between operations  3.05 us (8%)
  local copies, waits for them, and re-layouts  1.38 us (4%)
    pallas_call x1, Pallas kernels, on_device(): pl.pallas_call(functools.partial(kernel, sizes), out_shape=(jax.ShapeDtyp...  31.4 us
    unnamed x1, local copies, waits for them, and re-layouts  1.38 us

profile of v2, /device:TPU:1, one launch (start us, length us, event | category | flops | bytes accessed | tf_op | source)
XLA Modules:
  0.0 35.8 jit_solution(7912769995759508175)
XLA Ops:
  1.3 31.4 %shard_map.95 = (f32[1,1,2,2,16,128]{5,4,3,2,1,0:T(8,128)}, f32[1,1]{1,0:T(1,128)}) custom-call(f32[16,16,128]{2,1,0:T(8,128)} %cond_h.1, f32[16,16,128]{2,1,0:T(8,128)} %cond_v.1, f32[1,6,16,16,128]{4,3,2,1,0:T(8,128)} %fwd.1, f32[1,6,16,16,128]{4,3,2,1,0:T(8,128)} %adj.1, f32[1,4,1,1,2,32]{5,4,3,2,1,0:T(2,128)} %observed_in.1, ...), custom_call_target="tpu_custom_call" | custom-call | tf_op jit(solution)/shard_map/pallas_call | solution.py:405
  32.7 1.4 %copy.13 = f32[1,1,2,2,16,128]{5,4,3,2,1,0:T(8,128)} copy(f32[1,1,2,2,16,128]{5,4,3,2,1,0:T(8,128)} %get-tuple-element.8) | data formatting | bytes 65536

commit v3 on v2

--- a/solution.py
+++ b/solution.py
@@ -26,8 +26,9 @@
     out, misfit_out,
     fw, aw, cw, decay, drive, kept, grad, inj_own, inj_in, inj_win, obs_scr,
     observed, footprint, owner, rec_cells,
-    mis_own, mis_in, give, keep, got, part,
+    mis_own, mis_in, mis_tiles, mis_got, mis_chip, mis_part, give, keep, got, part,
     loc_sem, halo_send, halo_recv, inj_send, inj_recv, mis_send, mis_recv,
+    mis_sib_sem, mis_z_send, mis_z_recv,
     sib_send, sib_recv, z_send, z_recv,
 ):
     n_tx, n_gx, n_gy = sizes
@@ -181,8 +182,7 @@
 
     def span(j):
         if n_gx == 2:
-            rows = rows_w - j + j % 2
-            return jnp.where(has_lo, j - HALO, 0), rows // 2, 2
+            return jnp.where(has_lo, j - HALO, 0), rows_w - j, 1
         return start, 8, rows_w // 8
 
 
@@ -211,18 +211,19 @@
     def z_prev(f):
         return jnp.where(lane == 0, 0.0, pltpu.roll(f, 1, 1))
 
-    def step_rows(r, chunk, e_src, h, e_dst, after):
-        ex, ey, ez = (e_src[c, r] for c in range(3))
+    def step_rows(r, chunk, load, h, e_dst, after, keep_h):
+        ex, ey, ez = (load(c, r) for c in range(3))
         hp_y, hp_z = h[1, r - 1], h[2, r - 1]
         for i in range(chunk):
-            ey_n, ez_n = e_src[1, r + i + 1], e_src[2, r + i + 1]
-            ex_n = e_src[0, r + i + 1] if i < chunk - 1 else None
+            ey_n, ez_n = load(1, r + i + 1), load(2, r + i + 1)
+            ex_n = load(0, r + i + 1) if i < chunk - 1 else None
             hx = h[0, r + i] - half * ((y_next(ez) - ez) - (z_next(ey) - ey))
             hy = h[1, r + i] - half * ((z_next(ex) - ex) - (ez_n - ez))
             hz = h[2, r + i] - half * ((ey_n - ey) - (y_next(ex) - ex))
-            h[0, r + i] = hx
-            h[1, r + i] = hy
-            h[2, r + i] = hz
+            if keep_h:
+                h[0, r + i] = hx
+                h[1, r + i] = hy
+                h[2, r + i] = hz
             cx = (hz - y_prev(hz)) - (hy - z_prev(hy))
             cy = (hx - z_prev(hx)) - (hz - hp_z)
             cz = (hy - hp_y) - (hx - y_prev(hx))
@@ -236,19 +237,24 @@
                 after(r + i, new)
             ex, ey, ez = ex_n, ey_n, ez_n
 
-    def step(j, e_src, h, e_dst, after=None):
+    def step(j, load, h, e_dst, after=None):
         first, chunk, chunks = span(j)
 
         def body(k, carry):
-            step_rows(first + LOW + k * chunk, chunk, e_src, h, e_dst, after)
+            keep_h = j < STEPS - 1 or chunks > 1
+            step_rows(first + LOW + k * chunk, chunk, load, h, e_dst, after, keep_h)
             return carry
 
-        lax.fori_loop(0, chunks, body, 0)
+        if chunks == 1:
+            body(0, 0)
+        else:
+            lax.fori_loop(0, chunks, body, 0)
 
     wait_in(2)
     each_dir(lambda d: halo_copy(3, d).start(), to_side)
     for n in range(STEPS):
-        step(n, fw.at[0:3] if n == 0 else kept.at[n - 1], fw.at[3:6], kept.at[n])
+        e_src = fw if n == 0 else kept.at[n - 1]
+        step(n, lambda c, r, e=e_src: e[c, r], fw.at[3:6], kept.at[n])
 
     rec = jnp.zeros((size_y, depth), jnp.float32)
     for n in range(STEPS):
@@ -295,20 +301,49 @@
             inj_in[q * 3, size_y - 2 * HALO : size_y],
         )
 
+    def mis_sib():
+        return pltpu.make_async_remote_copy(
+            src_ref=mis_tiles, dst_ref=mis_got,
+            send_sem=mis_sib_sem.at[0], recv_sem=mis_sib_sem.at[1],
+            device_id=sibling, device_id_type=MESH,
+        )
+
+    def mis_z(dz):
+        return pltpu.make_async_remote_copy(
+            src_ref=mis_chip, dst_ref=mis_part.at[dz],
+            send_sem=mis_z_send.at[dz], recv_sem=mis_z_recv.at[dz],
+            device_id={"tx": 2 * z_partner(dz) + core}, device_id_type=MESH,
+        )
+
+    def misfit_round(n):
+        if n == STEPS - 1:
+            total = mis_own[...]
+            for k in range(1, n_gx * n_gy):
+                mis_copy(k).wait_recv()
+                total = total + mis_in[k]
+            mis_tiles[...] = total
+            mis_sib().start()
+        elif n == STEPS - 2:
+            mis_sib().wait_recv()
+            mis_chip[...] = mis_tiles[...] + mis_got[...]
+            for dz in range(1, nz):
+                mis_z(dz).start()
+        elif n == STEPS - 3:
+            total = mis_chip[...]
+            for dz in range(1, nz):
+                mis_z(dz).wait_recv()
+                total = total + mis_part[dz]
+            misfit_out[0, 0] = jnp.sum(total)
+
     for n in reversed(range(STEPS)):
-        first, chunk, chunks = span(STEPS - 1 - n)
-
-        def inject(k, carry, n=n, first=first, chunk=chunk):
-            for i in range(chunk):
-                x = first + k * chunk + i
-                plane = inj_win[(x + size_x) // size_x]
-                for c in range(2):
-                    at = (2 * n + c) * size_x + lax.rem(x + size_x, size_x)
-                    moved = pltpu.roll(plane, lax.rem(ZREC + depth - at, depth), 1)
-                    aw[c, x + LOW] = aw[c, x + LOW] + jnp.where(lane == ZREC, moved, 0.0)
-            return carry
-
-        lax.fori_loop(0, chunks, inject, 0)
+        def load(c, r, n=n):
+            e = aw[c, r]
+            if c == 2:
+                return e
+            x = r - LOW + size_x
+            at = (2 * n + c) * size_x + lax.rem(x, size_x)
+            moved = pltpu.roll(inj_win[x // size_x], lax.rem(ZREC + depth - at, depth), 1)
+            return e + jnp.where(lane == ZREC, moved, 0.0)
 
         def add_gradient(r, new, n=n):
             tile = slice(0, size_y)
@@ -320,17 +355,11 @@
             grad[0, r] = g_h
             grad[1, r] = g_v
 
-        step(STEPS - 1 - n, aw.at[0:3], aw.at[3:6], aw.at[0:3], add_gradient)
-
-    for k in range(1, n_gx * n_gy):
-        mis_copy(k).wait_recv()
-    misfit = mis_own[...]
-    for k in range(1, n_gx * n_gy):
-        misfit = misfit + mis_in[k]
+        step(STEPS - 1 - n, load, aw.at[3:6], aw.at[0:3], add_gradient)
+        misfit_round(n)
 
     flag = footprint[0, 0, 0].astype(jnp.float32)
     block = size_x // n_tx
-    cells_rows = 2 * block * size_y
 
     def ordered(dst, dz, to_core):
         z = z_partner(dz)
@@ -339,7 +368,6 @@
             for b in range(block):
                 at = (c * block + b) * size_y
                 dst[dz, at : at + size_y] = flag * grad[c, LOW + first + b]
-        dst[dz, cells_rows : cells_rows + 8] = misfit
 
     def sib_copy(dz):
         return pltpu.make_async_remote_copy(
@@ -375,13 +403,15 @@
         for b in range(block):
             at = (c * block + b) * size_y
             out[0, 0, c, b] = total[at : at + size_y]
-    misfit_out[0, 0] = jnp.sum(total[cells_rows : cells_rows + 8])
 
     for which in range(4):
         each_dir(lambda d, w=which: halo_copy(w, d).wait_send(), to_side)
     each_dir(lambda d: inj_copy(d).wait_send(), to_side)
     for k in range(1, n_gx * n_gy):
         mis_copy(k).wait_send()
+    mis_sib().wait_send()
+    for dz in range(1, nz):
+        mis_z(dz).wait_send()
     for dz in order:
         sib_copy(dz).wait_send()
     for dz in range(1, nz):
@@ -396,7 +426,7 @@
     rows = LOW + rows_w + 1
     wy = size_y + 2 * HALO
     block = size_x // n_tx
-    packed = 2 * block * size_y + 8
+    packed = 2 * block * size_y
     f32 = jnp.float32
     n_dirs = len(DIRS)
     plane = n_gx * n_gy
@@ -430,6 +460,10 @@
             vmem(rec_cells.shape, jnp.int32),
             vmem((8, depth), f32),
             vmem((plane, 8, depth), f32),
+            vmem((8, depth), f32),
+            vmem((8, depth), f32),
+            vmem((8, depth), f32),
+            vmem((nz, 8, depth), f32),
             vmem((nz, packed, depth), f32),
             vmem((nz, packed, depth), f32),
             vmem((nz, packed, depth), f32),
@@ -441,6 +475,9 @@
             dma((n_dirs,)),
             dma((plane,)),
             dma((plane,)),
+            dma((2,)),
+            dma((nz,)),
+            dma((nz,)),
             dma((nz,)),
             dma((nz,)),
             dma((nz,)),

time: 36 us -> 40.4 us (1.12)
  Pallas kernels: 31.4 us -> 35.8 us
    pallas_call x1, Pallas kernels: 31.4 us -> 35.8 us  [on_device(): pl.pallas_call(functools.partial(kernel, sizes), out_shape=(jax.ShapeDtyp...]
where the time goes in v3:
time: 40.4 us; the launch traced here: 40.2 us
  Pallas kernels  35.8 us (89%)
  between operations  3.05 us (8%)
  local copies, waits for them, and re-layouts  1.38 us (3%)
    pallas_call x1, Pallas kernels, on_device(): pl.pallas_call(functools.partial(kernel, sizes), out_shape=(jax.ShapeDtyp...  35.8 us
    unnamed x1, local copies, waits for them, and re-layouts  1.38 us

profile of v3, /device:TPU:1, one launch (start us, length us, event | category | flops | bytes accessed | tf_op | source)
XLA Modules:
  0.0 40.2 jit_solution(13134188889349784527)
XLA Ops:
  1.3 35.8 %shard_map.95 = (f32[1,1,2,2,16,128]{5,4,3,2,1,0:T(8,128)}, f32[1,1]{1,0:T(1,128)}) custom-call(f32[16,16,128]{2,1,0:T(8,128)} %cond_h.1, f32[16,16,128]{2,1,0:T(8,128)} %cond_v.1, f32[1,6,16,16,128]{4,3,2,1,0:T(8,128)} %fwd.1, f32[1,6,16,16,128]{4,3,2,1,0:T(8,128)} %adj.1, f32[1,4,1,1,2,32]{5,4,3,2,1,0:T(2,128)} %observed_in.1, ...), custom_call_target="tpu_custom_call" | custom-call | tf_op jit(solution)/shard_map/pallas_call | solution.py:435
  37.0 1.4 %copy.13 = f32[1,1,2,2,16,128]{5,4,3,2,1,0:T(8,128)} copy(f32[1,1,2,2,16,128]{5,4,3,2,1,0:T(8,128)} %get-tuple-element.8) | data formatting | bytes 65536

commit v4 on v3

--- a/solution.py
+++ b/solution.py
@@ -24,7 +24,7 @@
     sizes,
     cond_h, cond_v, fwd, adj, observed_in, footprint_in, owner_in, rec_in,
     out, misfit_out,
-    fw, aw, cw, decay, drive, kept, grad, inj_own, inj_in, inj_win, obs_scr,
+    fw, aw, cw, decay, drive, grad, inj_own, inj_in, inj_win, obs_scr,
     observed, footprint, owner, rec_cells,
     mis_own, mis_in, mis_tiles, mis_got, mis_chip, mis_part, give, keep, got, part,
     loc_sem, halo_send, halo_recv, inj_send, inj_recv, mis_send, mis_recv,
@@ -63,7 +63,7 @@
     locals_ = [
         pltpu.make_async_copy(cond_h, cw.at[0, tile_x, tile_y], loc_sem.at[0]),
         pltpu.make_async_copy(cond_v, cw.at[1, tile_x, tile_y], loc_sem.at[1]),
-        pltpu.make_async_copy(fwd.at[0], fw.at[:, tile_x, tile_y], loc_sem.at[2]),
+        pltpu.make_async_copy(fwd.at[0], fw.at[0:6, tile_x, tile_y], loc_sem.at[2]),
         pltpu.make_async_copy(adj.at[0], aw.at[:, tile_x, tile_y], loc_sem.at[3]),
         pltpu.make_async_copy(observed_in, observed, loc_sem.at[4]),
         pltpu.make_async_copy(rec_in, rec_cells, loc_sem.at[5]),
@@ -76,13 +76,13 @@
     rows_all = fw.shape[1]
     top = LOW + size_x
     for ref in (cw, fw, aw):
-        comps = ref.shape[0]
-        ref[:, :, size_y:wy] = jnp.zeros((comps, rows_all, wy - size_y, depth), jnp.float32)
+        comps = min(ref.shape[0], 6)
+        ref[0:comps, :, size_y:wy] = jnp.zeros((comps, rows_all, wy - size_y, depth), jnp.float32)
         if ref is cw and n_gx == 2:
             continue
         zero_rows = (LOW - 1, top) if n_gx == 2 else (*range(LOW), *range(top, rows_all))
         for r in zero_rows:
-            ref[:, r, 0:size_y] = jnp.zeros((comps, size_y, depth), jnp.float32)
+            ref[0:comps, r, 0:size_y] = jnp.zeros((comps, size_y, depth), jnp.float32)
     inj_in[...] = jnp.zeros_like(inj_in)
 
     barrier = pltpu.get_barrier_semaphore()
@@ -113,7 +113,7 @@
         src, dst = {
             0: (cond_h.at[sx, sy], cw.at[0, tx_, ty_]),
             1: (cond_v.at[sx, sy], cw.at[1, tx_, ty_]),
-            2: (fwd.at[0, :, sx, sy], fw.at[:, tx_, ty_]),
+            2: (fwd.at[0, :, sx, sy], fw.at[0:6, tx_, ty_]),
             3: (adj.at[0, :, sx, sy], aw.at[:, tx_, ty_]),
         }[which]
         return pltpu.make_async_remote_copy(
@@ -163,9 +163,9 @@
     count = jnp.dot(in_y, at_x, precision=highest, preferred_element_type=jnp.float32)
     obs_sum = jnp.dot(in_y, obs_l, precision=highest, preferred_element_type=jnp.float32)
 
-    for n in range(STEPS):
-        for x in sorted({size_x, size_x + HALO, rows_w}):
-            kept[n, :, LOW + x] = jnp.zeros((3, wy, depth), jnp.float32)
+    for x in sorted({size_x, size_x + HALO, rows_w}):
+        fw[6:, LOW + x] = jnp.zeros((3 * STEPS, wy, depth), jnp.float32)
+    grad[...] = jnp.zeros_like(grad)
 
     def wait_in(which):
         locals_[which].wait()
@@ -180,15 +180,12 @@
     y_ok = jnp.where(sub < size_y, 1.0, jnp.where(sub < size_y + HALO, y_hi, y_lo))
     half = STEP_DT * y_ok
 
-    def span(j):
-        if n_gx == 2:
-            return jnp.where(has_lo, j - HALO, 0), rows_w - j, 1
-        return start, 8, rows_w // 8
+    chunk = rows_w // 4
 
 
     def coefficients(k, carry):
-        for i in range(rows_w // 4):
-            x = start + k * (rows_w // 4) + i
+        for i in range(chunk):
+            x = start + k * chunk + i
             ok = y_ok * jnp.where(jnp.logical_or(x < size_x, has_hi), 1.0, 0.0)
             for c in range(2):
                 rate = 0.25 * cw[c, x + LOW]
@@ -211,7 +208,7 @@
     def z_prev(f):
         return jnp.where(lane == 0, 0.0, pltpu.roll(f, 1, 1))
 
-    def step_rows(r, chunk, load, h, e_dst, after, keep_h):
+    def step_rows(r, load, h, e_dst, after):
         ex, ey, ez = (load(c, r) for c in range(3))
         hp_y, hp_z = h[1, r - 1], h[2, r - 1]
         for i in range(chunk):
@@ -220,10 +217,9 @@
             hx = h[0, r + i] - half * ((y_next(ez) - ez) - (z_next(ey) - ey))
             hy = h[1, r + i] - half * ((z_next(ex) - ex) - (ez_n - ez))
             hz = h[2, r + i] - half * ((ey_n - ey) - (y_next(ex) - ex))
-            if keep_h:
-                h[0, r + i] = hx
-                h[1, r + i] = hy
-                h[2, r + i] = hz
+            h[0, r + i] = hx
+            h[1, r + i] = hy
+            h[2, r + i] = hz
             cx = (hz - y_prev(hz)) - (hy - z_prev(hy))
             cy = (hx - z_prev(hx)) - (hz - hp_z)
             cz = (hy - hp_y) - (hx - y_prev(hx))
@@ -237,32 +233,30 @@
                 after(r + i, new)
             ex, ey, ez = ex_n, ey_n, ez_n
 
-    def step(j, load, h, e_dst, after=None):
-        first, chunk, chunks = span(j)
-
+    def step(load, h, e_dst, after=None):
         def body(k, carry):
-            keep_h = j < STEPS - 1 or chunks > 1
-            step_rows(first + LOW + k * chunk, chunk, load, h, e_dst, after, keep_h)
+            step_rows(start + LOW + k * chunk, load, h, e_dst, after)
             return carry
 
-        if chunks == 1:
-            body(0, 0)
-        else:
-            lax.fori_loop(0, chunks, body, 0)
+        lax.fori_loop(0, 4, body, 0)
 
     wait_in(2)
     each_dir(lambda d: halo_copy(3, d).start(), to_side)
-    for n in range(STEPS):
-        e_src = fw if n == 0 else kept.at[n - 1]
-        step(n, lambda c, r, e=e_src: e[c, r], fw.at[3:6], kept.at[n])
-
-    rec = jnp.zeros((size_y, depth), jnp.float32)
-    for n in range(STEPS):
-        for c in range(2):
-            for x in range(size_x):
-                at = (2 * n + c) * size_x + x
-                e = kept[n, c, LOW + x, 0:size_y]
-                rec = jnp.where(lanes == at, pltpu.roll(e, (at - ZREC) % depth, 1), rec)
+    def forward(n, carry):
+        src, dst = jnp.where(n == 0, 0, 3 * n + 3), 3 * n + 6
+        step(lambda c, r: fw[src + c, r], fw.at[3:6], fw.at[pl.ds(dst, 3)])
+        return carry
+
+    lax.fori_loop(0, STEPS, forward, 0)
+
+    def records(k, rec):
+        for x in range(size_x):
+            at = k * size_x + x
+            e = fw[6 + 3 * (k // 2) + k % 2, LOW + x, 0:size_y]
+            rec = jnp.where(lanes == at, pltpu.roll(e, lax.rem(at + depth - ZREC, depth), 1), rec)
+        return rec
+
+    rec = lax.fori_loop(0, 2 * STEPS, records, jnp.zeros((size_y, depth), jnp.float32))
     inj_own[...] = count * rec - obs_sum
 
     def inj_copy(d):
@@ -316,27 +310,34 @@
         )
 
     def misfit_round(n):
-        if n == STEPS - 1:
+        @pl.when(n == STEPS - 1)
+        def _():
             total = mis_own[...]
             for k in range(1, n_gx * n_gy):
                 mis_copy(k).wait_recv()
                 total = total + mis_in[k]
             mis_tiles[...] = total
             mis_sib().start()
-        elif n == STEPS - 2:
+
+        @pl.when(n == STEPS - 2)
+        def _():
             mis_sib().wait_recv()
             mis_chip[...] = mis_tiles[...] + mis_got[...]
             for dz in range(1, nz):
                 mis_z(dz).start()
-        elif n == STEPS - 3:
+
+        @pl.when(n == STEPS - 3)
+        def _():
             total = mis_chip[...]
             for dz in range(1, nz):
                 mis_z(dz).wait_recv()
                 total = total + mis_part[dz]
             misfit_out[0, 0] = jnp.sum(total)
 
-    for n in reversed(range(STEPS)):
-        def load(c, r, n=n):
+    def adjoint(back, carry):
+        n = STEPS - 1 - back
+
+        def load(c, r):
             e = aw[c, r]
             if c == 2:
                 return e
@@ -345,18 +346,17 @@
             moved = pltpu.roll(inj_win[x // size_x], lax.rem(ZREC + depth - at, depth), 1)
             return e + jnp.where(lane == ZREC, moved, 0.0)
 
-        def add_gradient(r, new, n=n):
-            tile = slice(0, size_y)
-            g_h = new[0][tile] * kept[n, 0, r, tile] + new[1][tile] * kept[n, 1, r, tile]
-            g_v = new[2][tile] * kept[n, 2, r, tile]
-            if n < STEPS - 1:
-                g_h = grad[0, r] + g_h
-                g_v = grad[1, r] + g_v
-            grad[0, r] = g_h
-            grad[1, r] = g_v
-
-        step(STEPS - 1 - n, load, aw.at[3:6], aw.at[0:3], add_gradient)
+        def add_gradient(r, new):
+            stored = [fw[6 + 3 * n + c, r, 0:size_y] for c in range(3)]
+            mine = [f[0:size_y] for f in new]
+            grad[0, r] = grad[0, r] + mine[0] * stored[0] + mine[1] * stored[1]
+            grad[1, r] = grad[1, r] + mine[2] * stored[2]
+
+        step(load, aw.at[3:6], aw.at[0:3], add_gradient)
         misfit_round(n)
+        return carry
+
+    lax.fori_loop(0, STEPS, adjoint, 0)
 
     flag = footprint[0, 0, 0].astype(jnp.float32)
     block = size_x // n_tx
@@ -443,12 +443,11 @@
         ],
         out_specs=(pl.BlockSpec(memory_space=vmem), pl.BlockSpec(memory_space=smem)),
         scratch_shapes=[
-            vmem((6, rows, wy, depth), f32),
+            vmem((6 + 3 * STEPS, rows, wy, depth), f32),
             vmem((6, rows, wy, depth), f32),
             vmem((2, rows, wy, depth), f32),
             vmem((2, rows, wy, depth), f32),
             vmem((2, rows, wy, depth), f32),
-            vmem((STEPS, 3, rows, wy, depth), f32),
             vmem((2, rows, size_y, depth), f32),
             vmem((size_y, depth), f32),
             vmem((9, size_y, depth), f32),

time: 40.4 us -> 44.1 us (1.092)
  Pallas kernels: 35.8 us -> 39.4 us
    pallas_call x1, Pallas kernels: 35.8 us -> 39.4 us  [on_device(): pl.pallas_call(functools.partial(kernel, sizes), out_shape=(jax.ShapeDtyp...]
where the time goes in v4:
time: 44.1 us; the launch traced here: 43.9 us
  Pallas kernels  39.4 us (89%)
  between operations  3.05 us (7%)
  local copies, waits for them, and re-layouts  1.38 us (3%)
    pallas_call x1, Pallas kernels, on_device(): pl.pallas_call(functools.partial(kernel, sizes), out_shape=(jax.ShapeDtyp...  39.4 us
    unnamed x1, local copies, waits for them, and re-layouts  1.38 us

profile of v4, /device:TPU:1, one launch (start us, length us, event | category | flops | bytes accessed | tf_op | source)
XLA Modules:
  0.0 43.9 jit_solution(1769839178571715765)
XLA Ops:
  1.3 39.4 %shard_map.95 = (f32[1,1,2,2,16,128]{5,4,3,2,1,0:T(8,128)}, f32[1,1]{1,0:T(1,128)}) custom-call(f32[16,16,128]{2,1,0:T(8,128)} %cond_h.1, f32[16,16,128]{2,1,0:T(8,128)} %cond_v.1, f32[1,6,16,16,128]{4,3,2,1,0:T(8,128)} %fwd.1, f32[1,6,16,16,128]{4,3,2,1,0:T(8,128)} %adj.1, f32[1,4,1,1,2,32]{5,4,3,2,1,0:T(2,128)} %observed_in.1, ...), custom_call_target="tpu_custom_call" | custom-call | tf_op jit(solution)/shard_map/pallas_call | solution.py:435
  40.7 1.4 %copy.13 = f32[1,1,2,2,16,128]{5,4,3,2,1,0:T(8,128)} copy(f32[1,1,2,2,16,128]{5,4,3,2,1,0:T(8,128)} %get-tuple-element.8) | data formatting | bytes 65536

commit v5 on v2

--- a/solution.py
+++ b/solution.py
@@ -181,8 +181,8 @@
 
     def span(j):
         if n_gx == 2:
-            rows = rows_w - j + j % 2
-            return jnp.where(has_lo, j - HALO, 0), rows // 2, 2
+            gone = j - j % 2
+            return jnp.where(has_lo, gone - HALO, 0), (rows_w - gone) // 2, 2
         return start, 8, rows_w // 8
 
 
@@ -245,8 +245,8 @@
 
         lax.fori_loop(0, chunks, body, 0)
 
+    each_dir(lambda d: halo_copy(3, d).start(), to_side)
     wait_in(2)
-    each_dir(lambda d: halo_copy(3, d).start(), to_side)
     for n in range(STEPS):
         step(n, fw.at[0:3] if n == 0 else kept.at[n - 1], fw.at[3:6], kept.at[n])
 

time: 36 us -> 35.1 us (0.975)
  Pallas kernels: 31.4 us -> 30.5 us
    pallas_call x1, Pallas kernels: 31.4 us -> 30.5 us  [on_device(): pl.pallas_call(functools.partial(kernel, sizes), out_shape=(jax.ShapeDtyp...]
where the time goes in v5:
time: 35.1 us; the launch traced here: 34.9 us
  Pallas kernels  30.5 us (87%)
  between operations  3.05 us (9%)
  local copies, waits for them, and re-layouts  1.38 us (4%)
    pallas_call x1, Pallas kernels, on_device(): pl.pallas_call(functools.partial(kernel, sizes), out_shape=(jax.ShapeDtyp...  30.5 us
    unnamed x1, local copies, waits for them, and re-layouts  1.38 us

profile of v5, /device:TPU:1, one launch (start us, length us, event | category | flops | bytes accessed | tf_op | source)
XLA Modules:
  0.0 34.9 jit_solution(10725699199400991254)
XLA Ops:
  1.3 30.5 %shard_map.95 = (f32[1,1,2,2,16,128]{5,4,3,2,1,0:T(8,128)}, f32[1,1]{1,0:T(1,128)}) custom-call(f32[16,16,128]{2,1,0:T(8,128)} %cond_h.1, f32[16,16,128]{2,1,0:T(8,128)} %cond_v.1, f32[1,6,16,16,128]{4,3,2,1,0:T(8,128)} %fwd.1, f32[1,6,16,16,128]{4,3,2,1,0:T(8,128)} %adj.1, f32[1,4,1,1,2,32]{5,4,3,2,1,0:T(2,128)} %observed_in.1, ...), custom_call_target="tpu_custom_call" | custom-call | tf_op jit(solution)/shard_map/pallas_call | solution.py:405
  31.7 1.4 %copy.13 = f32[1,1,2,2,16,128]{5,4,3,2,1,0:T(8,128)} copy(f32[1,1,2,2,16,128]{5,4,3,2,1,0:T(8,128)} %get-tuple-element.8) | data formatting | bytes 65536

commit v6 on v5

--- a/solution.py
+++ b/solution.py
@@ -296,19 +296,12 @@
         )
 
     for n in reversed(range(STEPS)):
-        first, chunk, chunks = span(STEPS - 1 - n)
-
-        def inject(k, carry, n=n, first=first, chunk=chunk):
-            for i in range(chunk):
-                x = first + k * chunk + i
-                plane = inj_win[(x + size_x) // size_x]
-                for c in range(2):
-                    at = (2 * n + c) * size_x + lax.rem(x + size_x, size_x)
-                    moved = pltpu.roll(plane, lax.rem(ZREC + depth - at, depth), 1)
-                    aw[c, x + LOW] = aw[c, x + LOW] + jnp.where(lane == ZREC, moved, 0.0)
-            return carry
-
-        lax.fori_loop(0, chunks, inject, 0)
+        deep = n + 1
+        for x in range(-deep, size_x + deep):
+            for c in range(2):
+                at = (2 * n + c) * size_x + x % size_x
+                moved = pltpu.roll(inj_win[x // size_x + 1], (ZREC - at) % depth, 1)
+                aw[c, x + LOW] = aw[c, x + LOW] + jnp.where(lane == ZREC, moved, 0.0)
 
         def add_gradient(r, new, n=n):
             tile = slice(0, size_y)

time: 35.1 us -> 34.7 us (0.989)
  Pallas kernels: 30.5 us -> 30.1 us
    pallas_call x1, Pallas kernels: 30.5 us -> 30.1 us  [on_device(): pl.pallas_call(functools.partial(kernel, sizes), out_shape=(jax.ShapeDtyp...]
where the time goes in v6:
time: 34.7 us; the launch traced here: 34.5 us
  Pallas kernels  30.1 us (87%)
  between operations  3.05 us (9%)
  local copies, waits for them, and re-layouts  1.38 us (4%)
    pallas_call x1, Pallas kernels, on_device(): pl.pallas_call(functools.partial(kernel, sizes), out_shape=(jax.ShapeDtyp...  30.1 us
    unnamed x1, local copies, waits for them, and re-layouts  1.38 us

profile of v6, /device:TPU:1, one launch (start us, length us, event | category | flops | bytes accessed | tf_op | source)
XLA Modules:
  0.0 34.5 jit_solution(6628973958069544682)
XLA Ops:
  1.3 30.1 %shard_map.95 = (f32[1,1,2,2,16,128]{5,4,3,2,1,0:T(8,128)}, f32[1,1]{1,0:T(1,128)}) custom-call(f32[16,16,128]{2,1,0:T(8,128)} %cond_h.1, f32[16,16,128]{2,1,0:T(8,128)} %cond_v.1, f32[1,6,16,16,128]{4,3,2,1,0:T(8,128)} %fwd.1, f32[1,6,16,16,128]{4,3,2,1,0:T(8,128)} %adj.1, f32[1,4,1,1,2,32]{5,4,3,2,1,0:T(2,128)} %observed_in.1, ...), custom_call_target="tpu_custom_call" | custom-call | tf_op jit(solution)/shard_map/pallas_call | solution.py:398
  31.4 1.4 %copy.13 = f32[1,1,2,2,16,128]{5,4,3,2,1,0:T(8,128)} copy(f32[1,1,2,2,16,128]{5,4,3,2,1,0:T(8,128)} %get-tuple-element.8) | data formatting | bytes 65536
